TPU v7x, 32 devices: a whole 2x2x4 slice. The times are simulated.
32 devices in a mesh: var: 4 (over y, x), item: 8 (over z, core).
Axes of the slice: x: 2, y: 2, z: 4, core: 2. Of those that a mesh axis runs over, the one named last changes fastest.
Arguments:
- fields: bfloat16 [8, 12, 4, 2048], P('item', 'var'), may hold values from -6 to 6
- var_mask: int32 [8, 12], P('item'), may hold values from 0 to 1, as said below
- embed_weight: bfloat16 [12, 4, 1024], P('var'), may hold values from -3 to 3
- var_embed: bfloat16 [12, 1024], P('var'), may hold values from -6 to 6
- agg_query: bfloat16 [1024], replicated, may hold values from -6 to 6
- agg_key: bfloat16 [1024, 1024], replicated, may hold values from -0.1875 to 0.1875
- agg_value: bfloat16 [1024, 1024], replicated, may hold values from -0.1875 to 0.1875
- agg_out: bfloat16 [1024, 1024], replicated, may hold values from -0.375 to 0.375
- norm1_gain: float32 [1024], replicated, may hold values from 0.25 to 1.75
- norm1_bias: float32 [1024], replicated, may hold values from -3 to 3
- attn_qkv: bfloat16 [1024, 3072], replicated, may hold values from -0.1875 to 0.1875
- attn_proj: bfloat16 [1024, 1024], replicated, may hold values from -0.75 to 0.75
- norm2_gain: float32 [1024], replicated, may hold values from 0.25 to 1.75
- norm2_bias: float32 [1024], replicated, may hold values from -3 to 3
- mlp_in: bfloat16 [1024, 4096], replicated, may hold values from -0.1875 to 0.1875
- mlp_out: bfloat16 [4096, 1024], replicated, may hold values from -0.09375 to 0.09375
- cotangent: bfloat16 [8, 2048, 1024], P('item', 'var'), may hold values from -6 to 6
Outputs:
- output: bfloat16 [8, 2048, 1024], P('item', 'var')
- fields_grad: float32 [8, 12, 4, 2048], P('item', 'var')
- embed_weight_grad: float32 [12, 4, 1024], P('var', None, 'item')
- var_embed_grad: float32 [12, 1024], P('var', 'item')
- agg_query_grad: float32 [1024], P('item')
- agg_key_grad: float32 [1024, 1024], P('item')
- agg_value_grad: float32 [1024, 1024], P('item')
- agg_out_grad: float32 [1024, 1024], P('item')
- norm1_gain_grad: float32 [1024], P('item')
- norm1_bias_grad: float32 [1024], P('item')
- attn_qkv_grad: float32 [1024, 3072], P('item')
- attn_proj_grad: float32 [1024, 1024], P('item')
- norm2_gain_grad: float32 [1024], P('item')
- norm2_bias_grad: float32 [1024], P('item')
- mlp_in_grad: float32 [1024, 4096], P('item')
- mlp_out_grad: float32 [4096, 1024], P('item')
Inputs may be any that keep to these rules, and one draw needn't show every extreme that they name: `var_mask`: in every item at least 7 of the 12 slots are 1; which ones differs from item to item.
All inputs are finite; a program needn't handle non-finite values.
Results may differ from a plain program's by a relative error of at most 0.018.
Values may be sent and summed in bfloat16 or wider, within the bound.
No kernel may reach another device: no remote copies, remote signals or barrier semaphores. Data moves between devices by JAX's collectives and lax.ppermute only.
A program may use at most 448 MiB of HBM per device.

v0:
```python
from functools import partial

import jax
import jax.numpy as jnp
from jax import lax
from jax.sharding import PartitionSpec as P

HEADS = 16


epsilon = 1e-05
highest = lax.Precision.HIGHEST
masked_score = -1e30


def norm_forward(stream, norm_gain, norm_bias):
    centred = stream - jnp.mean(stream, axis=-1, keepdims=True)
    inverse = lax.rsqrt(jnp.mean(centred * centred, axis=-1, keepdims=True) + epsilon)
    unit_rows = centred * inverse
    return (unit_rows * norm_gain + norm_bias, unit_rows, inverse)


def norm_backward(upstream, unit_rows, inverse, norm_gain):
    scaled = upstream * norm_gain
    centred_grad = (
        scaled
        - jnp.mean(scaled, axis=-1, keepdims=True)
        - unit_rows * jnp.mean(scaled * unit_rows, axis=-1, keepdims=True)
    )
    return (
        centred_grad * inverse,
        jnp.sum(upstream * unit_rows, axis=(0, 1)),
        jnp.sum(upstream, axis=(0, 1)),
    )


def embed_tokens(pixels, tables, offsets):
    mixed = jnp.einsum("ivcp,vcd->ivpd", pixels, tables, preferred_element_type=jnp.float32)
    return (mixed + offsets.astype(jnp.float32)[None, :, None, :]).astype(jnp.bfloat16)


def attend(block_item):
    queries, key_rows, value_rows = block_item
    score_scale = queries.shape[-1] ** (-0.5)
    logits = (
        jnp.einsum("phe,khe->hpk", queries, key_rows, preferred_element_type=jnp.float32)
        * score_scale
    )
    attn_probs = jax.nn.softmax(logits, axis=-1).astype(jnp.bfloat16)
    return jnp.einsum(
        "hpk,khe->phe", attn_probs, value_rows, preferred_element_type=jnp.float32
    ).astype(jnp.bfloat16)


def attend_back(block_item):
    queries, key_rows, value_rows, upstream = block_item
    score_scale = queries.shape[-1] ** (-0.5)
    logits = (
        jnp.einsum("phe,khe->hpk", queries, key_rows, preferred_element_type=jnp.float32)
        * score_scale
    )
    probs_full = jax.nn.softmax(logits, axis=-1)
    attn_probs = probs_full.astype(jnp.bfloat16)
    g_probs = jnp.einsum("phe,khe->hpk", upstream, value_rows, preferred_element_type=jnp.float32)
    row_total = jnp.sum(g_probs * probs_full, axis=-1, keepdims=True)
    g_logits = (probs_full * (g_probs - row_total)).astype(jnp.bfloat16)
    g_queries = (
        jnp.einsum("hpk,khe->phe", g_logits, key_rows, preferred_element_type=jnp.float32)
        * score_scale
    )
    g_keys = (
        jnp.einsum("hpk,phe->khe", g_logits, queries, preferred_element_type=jnp.float32)
        * score_scale
    )
    g_values = jnp.einsum("hpk,phe->khe", attn_probs, upstream, preferred_element_type=jnp.float32)
    return (g_queries, g_keys, g_values)


def aggregate_back(query_keys, value_heads, block_item):
    tokens, probs_full, weights, pooled, g_values = block_item
    g_value_heads = jnp.einsum("phd,phe->dhe", pooled, g_values, preferred_element_type=jnp.float32)
    g_pooled = jnp.einsum(
        "phe,dhe->phd", g_values, value_heads, preferred_element_type=jnp.float32
    ).astype(jnp.bfloat16)
    g_weights = jnp.einsum("phd,vpd->phv", g_pooled, tokens, preferred_element_type=jnp.float32)
    row_total = jnp.sum(g_weights * probs_full, axis=-1, keepdims=True)
    g_scores = (probs_full * (g_weights - row_total)).astype(jnp.bfloat16)
    g_tokens = jnp.einsum("phv,phd->vpd", weights, g_pooled, preferred_element_type=jnp.float32)
    g_tokens = g_tokens + jnp.einsum(
        "phv,dh->vpd", g_scores, query_keys, preferred_element_type=jnp.float32
    )
    g_query_keys = jnp.einsum("vpd,phv->dh", tokens, g_scores, preferred_element_type=jnp.float32)
    return (g_tokens.astype(jnp.bfloat16), g_query_keys, g_value_heads)


def per_device(
    fields,
    var_mask,
    embed_weight,
    var_embed,
    agg_query,
    agg_key,
    agg_value,
    agg_out,
    norm1_gain,
    norm1_bias,
    attn_qkv,
    attn_proj,
    norm2_gain,
    norm2_bias,
    mlp_in,
    mlp_out,
    cotangent,
):
    model_width = agg_key.shape[0]
    head_count = HEADS
    head_size = model_width // head_count
    score_scale = head_size ** (-0.5)
    items_here = fields.shape[0]

    def split_heads(array):
        return array.reshape(array.shape[0], array.shape[1], head_count, head_size)

    key_heads = agg_key.reshape(model_width, head_count, head_size)
    value_heads = agg_value.reshape(model_width, head_count, head_size)
    query_heads = agg_query.reshape(head_count, head_size)
    query_keys = (
        jnp.einsum("dhe,he->dh", key_heads, query_heads, preferred_element_type=jnp.float32)
        * score_scale
    ).astype(jnp.bfloat16)
    tokens_var = embed_tokens(fields, embed_weight, var_embed)
    tokens = lax.all_to_all(tokens_var, "var", split_axis=2, concat_axis=1, tiled=True)
    scores = jnp.einsum("ivpd,dh->iphv", tokens, query_keys, preferred_element_type=jnp.float32)
    scores = jnp.where(var_mask[:, None, None, :] > 0, scores, masked_score)
    agg_probs = jax.nn.softmax(scores, axis=-1)
    agg_weights = agg_probs.astype(jnp.bfloat16)
    pooled = jnp.einsum(
        "iphv,ivpd->iphd", agg_weights, tokens, preferred_element_type=jnp.float32
    ).astype(jnp.bfloat16)
    agg_values = jnp.einsum(
        "iphd,dhe->iphe", pooled, value_heads, preferred_element_type=jnp.float32
    ).astype(jnp.bfloat16)
    agg_values = agg_values.reshape(items_here, -1, model_width)
    merged = jnp.einsum("ipd,de->ipe", agg_values, agg_out, preferred_element_type=jnp.float32)
    normed_full, unit_one, inverse_one = norm_forward(merged, norm1_gain, norm1_bias)
    normed = normed_full.astype(jnp.bfloat16)
    packed = jnp.einsum("ipd,de->ipe", normed, attn_qkv, preferred_element_type=jnp.float32).astype(
        jnp.bfloat16
    )
    queries = packed[:, :, :model_width]
    keys_local = packed[:, :, model_width : 2 * model_width]
    values_local = packed[:, :, 2 * model_width :]
    full_keys, full_values = (
        lax.all_gather(keys_local, "var", axis=1, tiled=True),
        lax.all_gather(values_local, "var", axis=1, tiled=True),
    )
    attended = lax.map(
        attend, (split_heads(queries), split_heads(full_keys), split_heads(full_values))
    )
    attended = attended.reshape(items_here, -1, model_width)
    stream = merged + jnp.einsum(
        "ipd,de->ipe", attended, attn_proj, preferred_element_type=jnp.float32
    )
    normed_two_full, unit_two, inverse_two = norm_forward(stream, norm2_gain, norm2_bias)
    normed_two = normed_two_full.astype(jnp.bfloat16)
    hidden = jnp.einsum("ipd,df->ipf", normed_two, mlp_in, preferred_element_type=jnp.float32)
    active = jax.nn.gelu(hidden, approximate=False).astype(jnp.bfloat16)
    output = (
        stream + jnp.einsum("ipf,fd->ipd", active, mlp_out, preferred_element_type=jnp.float32)
    ).astype(jnp.bfloat16)
    g_mlp_out = jnp.einsum("ipf,ipd->fd", active, cotangent, preferred_element_type=jnp.float32)
    g_active = jnp.einsum("ipd,fd->ipf", cotangent, mlp_out, preferred_element_type=jnp.float32)
    gelu_pullback = jax.vjp(lambda values_in: jax.nn.gelu(values_in, approximate=False), hidden)[1]
    g_hidden = gelu_pullback(g_active)[0].astype(jnp.bfloat16)
    g_mlp_in = jnp.einsum("ipd,ipf->df", normed_two, g_hidden, preferred_element_type=jnp.float32)
    g_normed_two = jnp.einsum(
        "ipf,df->ipd", g_hidden, mlp_in, preferred_element_type=jnp.float32
    ).astype(jnp.bfloat16)
    g_from_norm, g_norm2_gain, g_norm2_bias = norm_backward(
        g_normed_two.astype(jnp.float32), unit_two, inverse_two, norm2_gain
    )
    g_stream = cotangent.astype(jnp.float32) + g_from_norm
    g_attn_proj = jnp.einsum(
        "ipd,ipe->de", attended.astype(jnp.float32), g_stream, precision=highest
    )
    g_attended = jnp.einsum(
        "ipe,de->ipd", g_stream, attn_proj.astype(jnp.float32), precision=highest
    ).astype(jnp.bfloat16)
    full_keys, full_values = (
        lax.all_gather(keys_local, "var", axis=1, tiled=True),
        lax.all_gather(values_local, "var", axis=1, tiled=True),
    )
    g_queries, g_keys, g_values = lax.map(
        attend_back,
        (
            split_heads(queries),
            split_heads(full_keys),
            split_heads(full_values),
            split_heads(g_attended),
        ),
    )
    g_keys_mine, g_values_mine = (
        lax.psum_scatter(
            g_keys.reshape(items_here, -1, model_width).astype(jnp.bfloat16),
            "var",
            scatter_dimension=1,
            tiled=True,
        ).astype(jnp.float32),
        lax.psum_scatter(
            g_values.reshape(items_here, -1, model_width).astype(jnp.bfloat16),
            "var",
            scatter_dimension=1,
            tiled=True,
        ).astype(jnp.float32),
    )
    g_packed = jnp.concatenate(
        [g_queries.reshape(items_here, -1, model_width), g_keys_mine, g_values_mine], axis=-1
    ).astype(jnp.bfloat16)
    g_attn_qkv = jnp.einsum("ipd,ipe->de", normed, g_packed, preferred_element_type=jnp.float32)
    g_normed = jnp.einsum(
        "ipe,de->ipd", g_packed, attn_qkv, preferred_element_type=jnp.float32
    ).astype(jnp.bfloat16)
    g_from_first, g_norm1_gain, g_norm1_bias = norm_backward(
        g_normed.astype(jnp.float32), unit_one, inverse_one, norm1_gain
    )
    g_merged = g_stream + g_from_first
    g_agg_out = jnp.einsum(
        "ipd,ipe->de", agg_values.astype(jnp.float32), g_merged, precision=highest
    )
    g_agg_values = jnp.einsum(
        "ipe,de->ipd", g_merged, agg_out.astype(jnp.float32), precision=highest
    ).astype(jnp.bfloat16)
    agg_step = partial(aggregate_back, query_keys, value_heads)
    g_tokens, g_query_parts, g_value_parts = lax.map(
        agg_step, (tokens, agg_probs, agg_weights, pooled, split_heads(g_agg_values))
    )
    g_query_keys = jnp.sum(g_query_parts, axis=0)
    g_agg_value = jnp.sum(g_value_parts, axis=0).reshape(model_width, model_width)
    g_agg_key = (
        g_query_keys[:, :, None] * query_heads.astype(jnp.float32)[None, :, :] * score_scale
    ).reshape(model_width, model_width)
    g_agg_query = (
        jnp.einsum("dh,dhe->he", g_query_keys, key_heads.astype(jnp.float32), precision=highest)
        * score_scale
    ).reshape(model_width)
    g_tokens_var = lax.all_to_all(g_tokens, "var", split_axis=1, concat_axis=2, tiled=True)
    fields_grad = jnp.einsum(
        "ivpd,vcd->ivcp", g_tokens_var, embed_weight, preferred_element_type=jnp.float32
    )
    g_embed = jnp.einsum("ivcp,ivpd->vcd", fields, g_tokens_var, preferred_element_type=jnp.float32)
    g_var_embed = jnp.sum(g_tokens_var, axis=(0, 2), dtype=jnp.float32)
    (
        r_query,
        r_key,
        r_value,
        r_out,
        r_gain_one,
        r_bias_one,
        r_qkv,
        r_proj,
        r_gain_two,
        r_bias_two,
        r_mlp_in,
        r_mlp_out,
        embed_weight_grad,
        var_embed_grad,
    ) = (
        lax.psum_scatter(
            g_agg_query.astype(jnp.bfloat16), "item", scatter_dimension=0, tiled=True
        ).astype(jnp.float32),
        lax.psum_scatter(
            g_agg_key.astype(jnp.bfloat16), "item", scatter_dimension=0, tiled=True
        ).astype(jnp.float32),
        lax.psum_scatter(
            g_agg_value.astype(jnp.bfloat16), "item", scatter_dimension=0, tiled=True
        ).astype(jnp.float32),
        lax.psum_scatter(
            g_agg_out.astype(jnp.bfloat16), "item", scatter_dimension=0, tiled=True
        ).astype(jnp.float32),
        lax.psum_scatter(
            g_norm1_gain.astype(jnp.bfloat16), "item", scatter_dimension=0, tiled=True
        ).astype(jnp.float32),
        lax.psum_scatter(
            g_norm1_bias.astype(jnp.bfloat16), "item", scatter_dimension=0, tiled=True
        ).astype(jnp.float32),
        lax.psum_scatter(
            g_attn_qkv.astype(jnp.bfloat16), "item", scatter_dimension=0, tiled=True
        ).astype(jnp.float32),
        lax.psum_scatter(
            g_attn_proj.astype(jnp.bfloat16), "item", scatter_dimension=0, tiled=True
        ).astype(jnp.float32),
        lax.psum_scatter(
            g_norm2_gain.astype(jnp.bfloat16), "item", scatter_dimension=0, tiled=True
        ).astype(jnp.float32),
        lax.psum_scatter(
            g_norm2_bias.astype(jnp.bfloat16), "item", scatter_dimension=0, tiled=True
        ).astype(jnp.float32),
        lax.psum_scatter(
            g_mlp_in.astype(jnp.bfloat16), "item", scatter_dimension=0, tiled=True
        ).astype(jnp.float32),
        lax.psum_scatter(
            g_mlp_out.astype(jnp.bfloat16), "item", scatter_dimension=0, tiled=True
        ).astype(jnp.float32),
        lax.psum_scatter(
            g_embed.astype(jnp.bfloat16), "item", scatter_dimension=2, tiled=True
        ).astype(jnp.float32),
        lax.psum_scatter(
            g_var_embed.astype(jnp.bfloat16), "item", scatter_dimension=1, tiled=True
        ).astype(jnp.float32),
    )
    (
        t_query,
        t_key,
        t_value,
        t_out,
        t_gain_one,
        t_bias_one,
        t_qkv,
        t_proj,
        t_gain_two,
        t_bias_two,
        t_mlp_in,
        t_mlp_out,
    ) = (
        lax.psum(r_query.astype(jnp.bfloat16), "var").astype(jnp.float32),
        lax.psum(r_key.astype(jnp.bfloat16), "var").astype(jnp.float32),
        lax.psum(r_value.astype(jnp.bfloat16), "var").astype(jnp.float32),
        lax.psum(r_out.astype(jnp.bfloat16), "var").astype(jnp.float32),
        lax.psum(r_gain_one.astype(jnp.bfloat16), "var").astype(jnp.float32),
        lax.psum(r_bias_one.astype(jnp.bfloat16), "var").astype(jnp.float32),
        lax.psum(r_qkv.astype(jnp.bfloat16), "var").astype(jnp.float32),
        lax.psum(r_proj.astype(jnp.bfloat16), "var").astype(jnp.float32),
        lax.psum(r_gain_two.astype(jnp.bfloat16), "var").astype(jnp.float32),
        lax.psum(r_bias_two.astype(jnp.bfloat16), "var").astype(jnp.float32),
        lax.psum(r_mlp_in.astype(jnp.bfloat16), "var").astype(jnp.float32),
        lax.psum(r_mlp_out.astype(jnp.bfloat16), "var").astype(jnp.float32),
    )
    return (
        output,
        fields_grad,
        embed_weight_grad,
        var_embed_grad,
        t_query,
        t_key,
        t_value,
        t_out,
        t_gain_one,
        t_bias_one,
        t_qkv,
        t_proj,
        t_gain_two,
        t_bias_two,
        t_mlp_in,
        t_mlp_out,
    )


def solution(mesh):
    return jax.shard_map(
        per_device,
        mesh=mesh,
        in_specs=(
            P("item", "var", None, None),
            P("item", None),
            P("var", None, None),
            P("var", None),
            P(),
            P(),
            P(),
            P(),
            P(),
            P(),
            P(),
            P(),
            P(),
            P(),
            P(),
            P(),
            P("item", "var", None),
        ),
        out_specs=(
            P("item", "var", None),
            P("item", "var", None, None),
            P("var", None, "item"),
            P("var", "item"),
            P("item"),
            P("item", None),
            P("item", None),
            P("item", None),
            P("item"),
            P("item"),
            P("item", None),
            P("item", None),
            P("item"),
            P("item"),
            P("item", None),
            P("item", None),
        ),
        check_vma=False,
    )
```

profile of v0, /device:TPU:0, one launch (start us, length us, event | category | flops | bytes accessed | tf_op | source)
XLA Modules:
  0.0 1371.3 jit_solution(3949721838401060165)
XLA Ops:
  17.3 27.5 %copy.84 = bf16[1,3,2048,1024]{3,1,0,2:T(4,128)(2,1)} copy(bf16[1,3,2048,1024]{2,3,1,0:T(8,128)(2,1)} %fusion.23) | data formatting | bytes 25165824 | tf_op jit(solution)/shard_map/convert_element_type | solution.py:39
  61.9 173.8 %all-to-all-done = bf16[1,3,2048,1024]{3,1,0,2:T(4,128)(2,1)} async-done(((bf16[1,3,2048,1024]{3,1,0,2:T(4,128)(2,1)}), bf16[1,3,2048,1024]{3,1,0,2:T(4,128)(2,1)}, u32[]{:S(2)}, u32[]{:S(2)}) %all-to-all-start) | async-done | bytes 12582944 | tf_op jit(solution)/shard_map/all_to_all | solution.py:132
  235.7 11.7 copy.85
  256.1 29.9 %fusion.24 = bf16[512,16,1024]{2,1,0:T(8,128)(2,1)} fusion(bf16[512,16,12]{1,2,0:T(8,128)(2,1)} %copy.96, bf16[12,512,1024]{2,1,0:T(8,128)(2,1)} %bitcast.204), kind=kOutput, calls=%fused_computation.31 | convolution fusion | flops 209715200 | bytes 29556736 | tf_op jit(solution)/shard_map/iphv,ivpd->iphd/dot_general | solution.py:137
  286.0 17.6 %fusion.72 = bf16[16,512,64]{1,2,0:T(8,128)(2,1)S(1)} fusion(bf16[1024,16,64]{0,2,1:T(8,128)(2,1)} %bitcast.214, bf16[512,16,1024]{2,1,0:T(8,128)(2,1)} %fusion.24), kind=kOutput, calls=%fused_computation.100 | convolution fusion | flops 1074266112 | bytes 19922944 | tf_op jit(solution)/shard_map/iphd,dhe->iphe/dot_general | solution.py:140
  316.7 50.8 %all-gather.5.cloned.1.call-done = bf16[1,2048,1024]{2,1,0:T(8,128)(2,1)} async-done(((bf16[1,512,1024]{2,1,0:T(8,128)(2,1)}), bf16[1,2048,1024]{2,1,0:T(8,128)(2,1)}) %all-gather.5.cloned.1.call-update) | async-done | bytes 4194320 | tf_op jit(solution)/shard_map/all_gather | solution.py:154
  374.0 28.1 %fusion.113 = (f32[16,512]{1,0:T(8,128)S(1)}, f32[16,512,2048]{2,1,0:T(8,128)}) fusion(bf16[512,16,64]{0,2,1:T(8,128)(2,1)S(1)} %bitcast.218, bf16[2048,16,64]{0,2,1:T(8,128)(2,1)} %bitcast.211), kind=kOutput, calls=%fused_computation.150 | convolution fusion | flops 2197817344 | bytes 72384512 | tf_op jit(solution)/shard_map/while/body/eval_jaxpr/sub | solution.py:49
  402.1 20.0 %all-gather.3.cloned.1.call-done = bf16[1,2048,1024]{2,1,0:T(8,128)(2,1)} async-done(((bf16[1,512,1024]{2,1,0:T(8,128)(2,1)}), bf16[1,2048,1024]{2,1,0:T(8,128)(2,1)}) %all-gather.3.cloned.1.call-update) | async-done | bytes 4194320 | tf_op jit(solution)/shard_map/all_gather | solution.py:155
  428.6 24.9 %fusion.75 = bf16[16,64,512]{2,1,0:T(8,128)(2,1)S(1)} fusion(bf16[2048,16,64]{0,2,1:T(8,128)(2,1)} %bitcast.223, f32[16,512,2048]{2,1,0:T(8,128)} %get-tuple-element.153, f32[16,512]{1,0:T(8,128)S(1)} %get-tuple-element.152), kind=kOutput, calls=%fused_computation.101 | convolution fusion | flops 2181562368 | bytes 72384512 | tf_op jit(solution)/shard_map/while/body/eval_jaxpr/hpk,khe->phe/dot_general | solution.py:50
  457.3 28.0 %multiply_convert_fusion.2 = (bf16[512,4096]{1,0:T(8,128)(2,1)}, f32[512,4096]{1,0:T(8,128)}, f32[512,4096]{1,0:T(8,128)}) fusion(bf16[1024,4096]{1,0:T(8,128)(2,1)} %param.31, f32[512,1024]{1,0:T(8,128)S(1)} %get-tuple-element.155, f32[1024]{0:T(1024)S(1)} %copy-done.55, f32[1024]{0:T(1024)S(1)} %copy-done.51, f32[512]{0:T(512)S(1)} %add_rsqrt_fusion, ...), kind=kOutput, calls=%fused_computation.35 | convolution fusion | flops 4433903616 | bytes 31469568 | tf_op jit(solution)/shard_map/ipd,df->ipf/dot_general | solution.py:166
  485.3 13.3 add_convert_fusion
  498.5 10.4 fusion.54
  515.3 24.6 %fusion.40 = bf16[16,64,2048]{2,1,0:T(8,128)(2,1)} fusion(bf16[512,16,64]{0,2,1:T(8,128)(2,1)S(1)} %bitcast.231, f32[16,512,2048]{2,1,0:T(8,128)} %get-tuple-element.153, f32[16,512]{1,0:T(8,128)S(1)} %get-tuple-element.152), kind=kOutput, calls=%fused_computation.58 | convolution fusion | flops 2183135232 | bytes 72384512 | tf_op jit(solution)/shard_map/while/body/eval_jaxpr/hpk,phe->khe/dot_general | solution.py:75
  539.9 44.5 %multiply_reduce_fusion = (f32[16,512]{1,0:T(8,128)S(1)}, f32[16,512,2048]{2,1,0:T(8,128)}) fusion(f32[16,512,2048]{2,1,0:T(8,128)} %get-tuple-element.153, f32[16,512]{1,0:T(8,128)S(1)} %get-tuple-element.152, bf16[512,16,64]{0,2,1:T(8,128)(2,1)S(1)} %bitcast.232, bf16[2048,16,64]{0,2,1:T(8,128)(2,1)} %bitcast.224), kind=kOutput, calls=%fused_computation.2 | convolution fusion | flops 2197807104 | bytes 139526144 | tf_op jit(solution)/shard_map/while/body/eval_jaxpr/phe,khe->hpk/dot_general | solution.py:64
  584.5 55.1 %multiply_convert_fusion = bf16[16,512,2048]{2,1,0:T(8,128)(2,1)} fusion(f32[16,512,2048]{2,1,0:T(8,128)} %get-tuple-element.159, f32[16,512]{1,0:T(8,128)S(1)} %get-tuple-element.158, f32[16,512,2048]{2,1,0:T(8,128)} %get-tuple-element.153, f32[16,512]{1,0:T(8,128)S(1)} %get-tuple-element.152), kind=kLoop, calls=%fused_computation.1 | loop fusion | flops 67108864 | bytes 167837696 | tf_op jit(solution)/shard_map/while/body/eval_jaxpr/convert_element_type | solution.py:66
  639.6 18.4 %multiply_convert_fusion.1 = bf16[16,64,2048]{2,1,0:T(8,128)(2,1)} fusion(bf16[512,16,64]{0,2,1:T(8,128)(2,1)S(1)} %bitcast.219, bf16[16,512,2048]{2,1,0:T(8,128)(2,1)} %multiply_convert_fusion), kind=kOutput, calls=%fused_computation.33 | convolution fusion | flops 2151677952 | bytes 38797312 | tf_op jit(solution)/shard_map/while/body/eval_jaxpr/hpk,phe->khe/dot_general | solution.py:72
  658.2 18.3 %multiply_convert_fusion.3 = bf16[16,64,512]{2,1,0:T(8,128)(2,1)S(1)} fusion(bf16[2048,16,64]{0,2,1:T(8,128)(2,1)} %bitcast.212, bf16[16,512,2048]{2,1,0:T(8,128)(2,1)} %multiply_convert_fusion), kind=kOutput, calls=%fused_computation.88 | convolution fusion | flops 2148532224 | bytes 38797312 | tf_op jit(solution)/shard_map/while/body/eval_jaxpr/hpk,khe->phe/dot_general | solution.py:68
  676.5 34.4 %reduce-scatter.18.cloned.1.call-done = bf16[1,512,1024]{1,2,0:T(8,128)(2,1)} async-done(((bf16[1,2048,1024]{1,2,0:T(8,128)(2,1)}), bf16[1,512,1024]{1,2,0:T(8,128)(2,1)}) %reduce-scatter.18.cloned.1.call-update) | async-done | bytes 1048592 | tf_op jit(solution)/shard_map/reduce_scatter | solution.py:203
  727.4 9.9 convert_bitcast_fusion
  737.3 29.4 %fusion.7 = f32[512,16,12]{1,2,0:T(8,128)} fusion(bf16[12,512,1024]{2,1,0:T(8,128)(2,1)} %bitcast.205, bf16[512,16,1024]{2,0,1:T(8,128)(2,1)} %convert_bitcast_fusion), kind=kOutput, calls=%fused_computation.12 | convolution fusion | flops 201326592 | bytes 29753344 | tf_op jit(solution)/shard_map/while/body/eval_jaxpr/phd,vpd->phv/dot_general | solution.py:85
  792.7 25.3 %fusion.66 = bf16[16,64,1024]{2,1,0:T(8,128)(2,1)} fusion(bf16[512,16,64]{0,2,1:T(8,128)(2,1)S(1)} %bitcast.221, bf16[512,16,1024]{2,1,0:T(8,128)(2,1)} %fusion.24), kind=kOutput, calls=%fused_computation.96 | convolution fusion | flops 1074790400 | bytes 19922944 | tf_op jit(solution)/shard_map/while/body/eval_jaxpr/phd,phe->dhe/dot_general | solution.py:81
  828.9 10.9 convolution_convert_fusion.1
  860.5 10.4 fusion.100
  870.8 32.1 %copy.101 = f32[1024,512,12]{0,2,1:T(8,128)} copy(f32[1024,512,12]{1,0,2:T(8,128)} %fusion.100) | data formatting | bytes 50331648 | tf_op jit(solution)/shard_map/while/body/eval_jaxpr/phv,dh->vpd/dot_general | solution.py:89
  902.9 24.9 %fusion.11 = bf16[1,12,512,1024]{3,1,2,0:T(8,128)(2,1)} fusion(f32[1024,512,12]{0,2,1:T(8,128)} %copy.101, bf16[512,16,12]{1,2,0:T(8,128)(2,1)S(1)} %copy-done.4, bf16[512,16,1024]{2,0,1:T(8,128)(2,1)} %convert_bitcast_fusion), kind=kOutput, calls=%fused_computation.16 | convolution fusion | flops 213909504 | bytes 54722560 | tf_op jit(solution)/shard_map/while/body/eval_jaxpr/phv,phd->vpd/dot_general | solution.py:88
  927.8 12.5 copy.102
  940.4 141.2 %all_to_all.30 = bf16[1,12,512,1024]{3,2,0,1:T(8,128)(2,1)S(1)} all-to-all(bf16[1,12,512,1024]{3,2,0,1:T(8,128)(2,1)S(1)} %copy.102), channel_id=1, replica_groups=mesh['var'=4,'item'=8] {'var'}, dimensions={1} | all-to-all | bytes 25165824 | tf_op jit(solution)/shard_map/all_to_all | solution.py:246
  1113.0 70.5 %reduce-scatter.26.cloned.1.call-done = bf16[128,3072]{1,0:T(8,128)(2,1)} async-done(((bf16[1024,3072]{1,0:T(8,128)(2,1)}), bf16[128,3072]{1,0:T(8,128)(2,1)}) %reduce-scatter.26.cloned.1.call-update) | async-done | bytes 786448 | tf_op jit(solution)/shard_map/reduce_scatter | solution.py:286
  1185.1 10.8 fusion.81
  1197.9 25.9 %all-reduce.5 = (bf16[1024]{0:T(1024)(128)(2,1)S(1)}, bf16[1024]{0:T(1024)(128)(2,1)S(1)}, bf16[1024]{0:T(1024)(128)(2,1)S(1)}, bf16[1024]{0:T(1024)(128)(2,1)S(1)}, bf16[1024]{0:T(1024)(128)(2,1)S(1)}) all-reduce(bf16[1024]{0:T(1024)(128)(2,1)S(1)} %convert_element_type.331, ...), channel_id=6, replica_groups=mesh['var'=4,'item'=8] {'item'}, use_global_device_ids=true, to_apply=%region_19.20.clone | all-reduce | flops 5120 | bytes 20480
  1224.2 9.8 all-reduce.6
  1248.4 102.1 %all-reduce.10.cloned.1.call-done = (bf16[128,1024]{0,1:T(8,128)(2,1)}, bf16[128,1024]{1,0:T(8,128)(2,1)}, bf16[128,1024]{1,0:T(8,128)(2,1)}, bf16[128,3072]{1,0...) async-done(((bf16[128,1024]{0,1:T(8,128)(2,1)}, bf16[128,1024]{1,0:T(8,128)(2,1)}, bf16[128,1024]{1,0:T(8,128)(2,1)}, ...) | async-done | bytes 3932176 | tf_op jit(solution)/shard_map/psum | solution.py:326
  (246 shorter events, 208.9 us)
Async XLA Ops:
  7.2 446.4 %copy-start = (bf16[1024,1024]{1,0:T(8,128)(2,1)S(1)}, bf16[1024,1024]{1,0:T(8,128)(2,1)}, u32[]{:S(2)}) copy-start(bf16[1024,1024]{1,0:T(8,128)(2,1)} %param.28) | copy-start | bytes 6291460
  44.8 190.9 %all-to-all-start = ((bf16[1,3,2048,1024]{3,1,0,2:T(4,128)(2,1)}), bf16[1,3,2048,1024]{3,1,0,2:T(4,128)(2,1)}, u32[]{:S(2)}, u32[]{:S(2)}) async-start(bf16[1,3,2048,1024]{3,1,0,2:T(4,128)(2,1)} %copy.84), calls=%async_computation | async-start | bytes 33554432 | tf_op jit(solution)/shard_map/all_to_all | solution.py:132
  51.9 315.6 %all-gather.5.cloned.1.call-start = ((), (), s32[]{:S(2)}) async-start(), calls=%async_computation.14 | async-start | bytes 5242880 | tf_op jit(solution)/shard_map/all_gather | solution.py:154
  61.9 185.5 %copy-start.32 = (f32[16,1,1024]{2,1,0:T(1,128)}, f32[16,1,1024]{2,1,0:T(1,128)S(1)}, u32[]{:S(2)}) copy-start(f32[16,1,1024]{2,1,0:T(1,128)S(1)} %fusion.115) | copy-start | bytes 196612
  314.2 107.9 %all-gather.3.cloned.1.call-start = ((), (), s32[]{:S(2)}) async-start(), calls=%async_computation.13 | async-start | bytes 5242880 | tf_op jit(solution)/shard_map/all_gather | solution.py:155
  314.9 361.6 %reduce-scatter.20.cloned.1.call-start = ((), (), s32[]{:S(2)}) async-start(), calls=%async_computation.16 | async-start | bytes 5242880 | tf_op jit(solution)/shard_map/reduce_scatter | solution.py:209
  316.7 85.4 %copy-start.13 = (bf16[1,512,1024]{1,2,0:T(8,128)(2,1)}, bf16[1,512,1024]{1,2,0:T(8,128)(2,1)S(1)}, u32[]{:S(2)}) copy-start(bf16[1,512,1024]{1,2,0:T(8,128)(2,1)S(1)} %copy.91) | copy-start | bytes 3145732
  456.9 52.1 %copy-start.10 = (f32[512,1024]{1,0:T(8,128)}, f32[512,1024]{1,0:T(8,128)S(1)}, u32[]{:S(2)}) copy-start(f32[512,1024]{1,0:T(8,128)S(1)} %get-tuple-element.155) | copy-start | bytes 6291460
  456.9 52.1 %copy-start.39 = (f32[512]{0:T(512)}, f32[512]{0:T(512)S(1)}, u32[]{:S(2)}) copy-start(f32[512]{0:T(512)S(1)} %broadcast_multiply_fusion.4) | copy-start | bytes 6148
  457.3 51.7 %copy-start.43 = (f32[512]{0:T(512)}, f32[512]{0:T(512)S(1)}, u32[]{:S(2)}) copy-start(f32[512]{0:T(512)S(1)} %add_rsqrt_fusion) | copy-start | bytes 6148
  584.4 126.5 %reduce-scatter.18.cloned.1.call-start = ((), (), s32[]{:S(2)}) async-start(), calls=%async_computation.15 | async-start | bytes 5242880 | tf_op jit(solution)/shard_map/reduce_scatter | solution.py:203
  584.4 55.1 %copy-start.14 = (bf16[1,512,1024]{1,2,0:T(8,128)(2,1)S(1)}, bf16[1,512,1024]{1,2,0:T(8,128)(2,1)}, u32[]{:S(2)}) copy-start(bf16[1,512,1024]{1,2,0:T(8,128)(2,1)} %copy-done.13) | copy-start | bytes 3145732
  658.0 451.2 %reduce-scatter.38.cloned.1.call-start = ((), (), s32[]{:S(2)}) async-start(), calls=%async_computation.25 | async-start | bytes 2359296
  658.1 52.8 %copy-start.6 = (f32[512,1024]{1,0:T(8,128)S(1)}, f32[512,1024]{1,0:T(8,128)}, u32[]{:S(2)}) copy-start(f32[512,1024]{1,0:T(8,128)} %copy-done.5) | copy-start | bytes 6291460
  658.1 52.8 %copy-start.42 = (f32[512]{0:T(512)S(1)}, f32[512]{0:T(512)}, u32[]{:S(2)}) copy-start(f32[512]{0:T(512)} %copy-done.41) | copy-start | bytes 6148
  658.1 52.8 %copy-start.48 = (f32[512]{0:T(512)S(1)}, f32[512]{0:T(512)}, u32[]{:S(2)}) copy-start(f32[512]{0:T(512)} %copy-done.47) | copy-start | bytes 6148
  658.1 52.8 %copy-start.50 = (f32[1024]{0:T(1024)S(1)}, f32[1024]{0:T(1024)}, u32[]{:S(2)}) copy-start(f32[1024]{0:T(1024)} %param.25) | copy-start | bytes 12292
  676.5 42.7 %copy-start.27 = (bf16[16,64,512]{2,1,0:T(8,128)(2,1)}, bf16[16,64,512]{2,1,0:T(8,128)(2,1)S(1)}, u32[]{:S(2)}) copy-start(bf16[16,64,512]{2,1,0:T(8,128)(2,1)S(1)} %multiply_convert_fusion.3) | copy-start | bytes 3145732
  737.3 33.1 %copy-start.8 = (f32[1,512,16,12]{1,2,3,0:T(8,128)S(1)}, f32[1,512,16,12]{1,2,3,0:T(8,128)}, u32[]{:S(2)}) copy-start(f32[1,512,16,12]{1,2,3,0:T(8,128)} %copy-done.7) | copy-start | bytes 1179652
  785.4 325.7 %reduce-scatter.28.cloned.1.call-start = ((), (), s32[]{:S(2)}) async-start(), calls=%async_computation.20 | async-start | bytes 2359296 | tf_op jit(solution)/shard_map/reduce_scatter | solution.py:289
  792.2 318.8 %reduce-scatter.22.cloned.1.call-start = ((), (), s32[]{:S(2)}) async-start(), calls=%async_computation.17 | async-start | bytes 2359296 | tf_op jit(solution)/shard_map/reduce_scatter | solution.py:274
  822.2 288.9 %reduce-scatter.24.cloned.1.call-start = ((), (), s32[]{:S(2)}) async-start(), calls=%async_computation.18 | async-start | bytes 2359296 | tf_op jit(solution)/shard_map/reduce_scatter | solution.py:277
  828.6 282.5 %reduce-scatter.30.cloned.1.call-start = ((), (), s32[]{:S(2)}) async-start(), calls=%async_computation.21 | async-start | bytes 9437184 | tf_op jit(solution)/shard_map/reduce_scatter | solution.py:298
  839.8 273.2 %reduce-scatter.32.cloned.1.call-start = ((), (), s32[]{:S(2)}) async-start(), calls=%async_computation.22 | async-start | bytes 9437184 | tf_op jit(solution)/shard_map/reduce_scatter | solution.py:301
  850.2 333.4 %reduce-scatter.26.cloned.1.call-start = ((), (), s32[]{:S(2)}) async-start(), calls=%async_computation.19 | async-start | bytes 7077888 | tf_op jit(solution)/shard_map/reduce_scatter | solution.py:286
  859.6 385.8 %reduce-scatter.36.cloned.1.call-start = ((), (), s32[]{:S(2)}) async-start(), calls=%async_computation.24 | async-start | bytes 294912
  1100.6 146.2 %reduce-scatter.34.cloned.1.call-start = ((), (), s32[]{:S(2)}) async-start(), calls=%async_computation.23 | async-start | bytes 294912
  1107.2 76.4 %copy-start.61 = (u32[32]{0:T(128)S(1)}, u32[32]{0:T(128)}, u32[]{:S(2)}) copy-start(u32[32]{0:T(128)} %constant.165) | copy-start | bytes 388
  1107.2 77.6 %copy-start.16 = (bf16[512,1024]{1,0:T(8,128)(2,1)S(1)}, bf16[512,1024]{1,0:T(8,128)(2,1)}, u32[]{:S(2)}) copy-start(bf16[512,1024]{1,0:T(8,128)(2,1)} %copy-done.15) | copy-start | bytes 3145732
  1109.2 241.3 %all-reduce.10.cloned.1.call-start = ((), (), s32[]{:S(2)}) async-start(), calls=%async_computation.26 | async-start | bytes 7864320 | tf_op jit(solution)/shard_map/psum | solution.py:326
  1185.1 51.5 %copy-start.38 = (bf16[3,4,1024]{2,1,0:T(4,128)(2,1)S(1)}, bf16[3,4,1024]{2,1,0:T(4,128)(2,1)}, u32[]{:S(2)}) copy-start(bf16[3,4,1024]{2,1,0:T(4,128)(2,1)} %param.19) | copy-start | bytes 73732
  1236.6 128.0 %copy-start.1 = (bf16[1024,1024]{1,0:T(8,128)(2,1)S(1)}, bf16[1024,1024]{1,0:T(8,128)(2,1)}, u32[]{:S(2)}) copy-start(bf16[1024,1024]{1,0:T(8,128)(2,1)} %param.28) | copy-start | bytes 6291460
  (46 other events, 362.5 us)
Sparse Core Ops, SparseCore 0:
  314.3 53.1 all-gather.4
  369.3 52.7 all-gather.2
  584.5 52.6 reduce-scatter.19
  658.2 52.7 reduce-scatter.17
  785.5 35.7 reduce-scatter.37
  823.5 34.4 reduce-scatter.27
  860.3 34.5 reduce-scatter.21
  897.7 34.4 reduce-scatter.23
  934.6 88.2 reduce-scatter.29
  1025.0 87.9 reduce-scatter.31
  1115.4 68.1 reduce-scatter.25
  1186.2 28.7 reduce-scatter.35
  1217.9 28.5 reduce-scatter.33
  1250.8 99.6 all-reduce.9
where the time goes:
time: 1380 us; the launch traced here: 1370 us
  matrix products  475 us (34%)
  waiting for transfers between devices  455 us (33%)
  blocking collectives  177 us (13%)
  local copies, waits for them, and re-layouts  153 us (11%)
  other arithmetic  87.1 us (6%)
  between operations  15.5 us (1%)
    all_to_all x1, waiting for transfers between devices, per_device(): lax.all_to_all(tokens_var, 'var', split_axis=2, concat_axis=1, tiled=True)  174 us
    all_to_all x1, blocking collectives, per_device(): lax.all_to_all(g_tokens, 'var', split_axis=1, concat_axis=2, tiled=True)  141 us
    psum x1, waiting for transfers between devices, per_device(): lax.psum(r_key.astype(jnp.bfloat16), 'var').astype(jnp.float32)  102 us
    reduce_scatter x1, waiting for transfers between devices, per_device(): lax.psum_scatter(g_attn_qkv.astype(jnp.bfloat16), 'item', scatter_dimensi...  70.5 us
    convert_element_type x1, other arithmetic, attend_back(): g_logits = (probs_full * (g_probs - row_total)).astype(jnp.bfloat16)  55.1 us
    all_gather x1, waiting for transfers between devices, per_device(): lax.all_gather(keys_local, 'var', axis=1, tiled=True)  50.8 us
    dot_general x1, matrix products, attend_back(): jnp.einsum('phe,khe->hpk', upstream, value_rows, preferred_element_type=j...  44.5 us
    unnamed x143, local copies, waits for them, and re-layouts  34.6 us
  transfers between devices with their start and end apart: 15, of which 7 were waited for; matrix products, arithmetic and copies ran while one was open for 25% of the time, Pallas kernels for 0%

commit v1 on v0

v1 whole, which is shorter than its diff:
```python
from functools import partial

import jax
import jax.numpy as jnp
from jax import lax
from jax.experimental import pallas as pl
from jax.experimental.pallas import tpu as pltpu
from jax.sharding import Mesh
from jax.sharding import PartitionSpec as P

HEADS = 16
TABLES = 5

epsilon = 1e-05
masked_score = -1e30
highest = lax.Precision.HIGHEST
f32 = jnp.float32
bf16 = jnp.bfloat16
COST = 0.05
VMEM_BYTES = 56 * 1024 * 1024
LOG2E = 1.4426950408889634


def dot(a, b):
    return lax.dot_general(a, b, (((1,), (0,)), ((), ())), preferred_element_type=f32)


def dot_nt(a, b):
    return lax.dot_general(a, b, (((1,), (1,)), ((), ())), preferred_element_type=f32)


def dot_tn(a, b):
    return lax.dot_general(a, b, (((0,), (0,)), ((), ())), preferred_element_type=f32)


def split_two(wide):
    high = wide.astype(bf16)
    return high, (wide - high.astype(f32)).astype(bf16)


def split_three(wide):
    high, rest = split_two(wide)
    low = wide - high.astype(f32) - rest.astype(f32)
    return high, rest, low.astype(bf16)


def columns(parts, rows, width):
    lane = lax.broadcasted_iota(jnp.int32, (rows, width), 1)
    out = jnp.zeros((rows, width), f32)
    for i, part in enumerate(parts):
        out = jnp.where(lane == i, part.astype(f32), out)
    return out.astype(bf16)


def whole(shape):
    return pl.BlockSpec(shape, lambda *_: (0,) * len(shape))


def params(vmem=VMEM_BYTES):
    return pltpu.CompilerParams(vmem_limit_bytes=vmem)


def cost(flops, bytes_accessed, transcendentals=0, share=COST):
    return pl.CostEstimate(
        flops=int(flops * share), bytes_accessed=int(bytes_accessed * share), transcendentals=0
    )


def norm_parts(stream):
    centred = stream - jnp.mean(stream, axis=-1, keepdims=True)
    inverse = lax.rsqrt(jnp.mean(centred * centred, axis=-1, keepdims=True) + epsilon)
    return centred * inverse, inverse


def norm_back(upstream, unit_rows, inverse, gain):
    scaled = upstream * gain
    return inverse * (
        scaled
        - jnp.mean(scaled, axis=-1, keepdims=True)
        - unit_rows * jnp.mean(scaled * unit_rows, axis=-1, keepdims=True)
    )


def variable_probs(pixel_rows, score_high, score_low, real, slots):
    scores = dot(score_high, pixel_rows) + dot(score_low, pixel_rows)
    scores = scores.reshape(HEADS, slots, pixel_rows.shape[1])
    scores = jnp.where(real[None] > 0, scores, masked_score)
    powers = jnp.exp(scores - jnp.max(scores, axis=1, keepdims=True))
    return powers / jnp.sum(powers, axis=1, keepdims=True)


def prep_kernel(count, vars_here, patches, *refs):
    place_ref = refs[0]
    pieces = refs[1 : 1 + count]
    query_ref, key_ref, value_ref = refs[1 + count : 4 + count]
    (
        pix_ref, tables_ref, shi_ref, slo_ref, sthi_ref, stlo_ref, front_ref, back_ref, keys_ref,
        qk_ref, spread_ref, all_s,
    ) = refs[4 + count :]
    me = place_ref[0]
    depth, width = tables_ref.shape
    slots = depth // TABLES
    size = width // HEADS
    rows = TABLES * vars_here
    total = None
    for d in range(count):
        row = lax.broadcasted_iota(jnp.int32, (depth, rows), 0)
        col = lax.broadcasted_iota(jnp.int32, (depth, rows), 1)
        want = (col % TABLES) * slots + (me ^ d) * vars_here + col // TABLES
        part = dot(jnp.where(row == want, 1.0, 0.0).astype(bf16), pieces[d][...])
        total = part if total is None else total + part
    all_s[...] = total.astype(bf16)
    mine = patches // count
    for d in range(count):
        at = pl.multiple_of((me ^ d) * mine, mine)
        pix_ref[:, d * mine : (d + 1) * mine] = all_s[:, pl.ds(at, mine)]
    tables = all_s[:, patches:]
    tables_ref[...] = tables
    head = lax.broadcasted_iota(jnp.int32, (HEADS, width), 0)
    same = lax.broadcasted_iota(jnp.int32, (HEADS, width), 1) // size == head
    spread = jnp.where(same, query_ref[...].astype(f32), 0.0)
    scale = size ** (-0.5)
    spread_ref[...] = (spread * scale).astype(bf16)
    query_keys = (dot_nt(key_ref[...], spread.astype(bf16)) * scale).astype(bf16)
    qk_ref[...] = query_keys
    halves = split_two(dot(tables, query_keys))
    wide = HEADS * slots
    picks = lax.broadcasted_iota(jnp.int32, (wide, HEADS), 0) // slots
    picks = jnp.where(picks == lax.broadcasted_iota(jnp.int32, (wide, HEADS), 1), 1.0, 0.0).astype(bf16)
    for half, tall, flat in zip(halves, (shi_ref, slo_ref), (sthi_ref, stlo_ref)):
        row = lax.broadcasted_iota(jnp.int32, (wide, depth), 0) % slots
        col = lax.broadcasted_iota(jnp.int32, (wide, depth), 1) % slots
        tall[...] = jnp.where(row == col, dot_nt(picks, half), 0.0).astype(bf16)
        row = lax.broadcasted_iota(jnp.int32, (depth, wide), 0) % slots
        col = lax.broadcasted_iota(jnp.int32, (depth, wide), 1) % slots
        flat[...] = jnp.where(row == col, dot_nt(half, picks), 0.0).astype(bf16)
    mixed = dot(tables, value_ref[...])
    high, low = split_two(mixed)
    high_wide, low_wide = high.astype(f32), low.astype(f32)
    front_ref[...] = jnp.concatenate([high_wide, high_wide, low_wide], axis=0).T.astype(bf16)
    both = jnp.concatenate([high, low], axis=0)
    for h in range(HEADS):
        back_ref[h] = both[:, h * size : (h + 1) * size]
    keys_ref[...] = dot(tables, key_ref[...])


def front_kernel(
    own_blocks, n_z, place_ref, pix_ref, shi_ref, slo_ref, real_ref, ev_ref, out_w_ref, gain_ref,
    bias_ref, wq_ref, wk_ref, wv_ref,
    values_ref, merged_ref, send_ref, keep_ref, q_ref, k_ref, v_ref, flat_ref, tall_s,
):
    slots = real_ref.shape[0]
    pixel_rows = pix_ref[...]
    probs = variable_probs(pixel_rows, shi_ref[...], slo_ref[...], real_ref[...], slots)
    weights = probs.astype(bf16).astype(f32)
    pixels = pixel_rows.astype(f32).reshape(TABLES, slots, -1)
    size = ev_ref.shape[0] // HEADS
    for h in range(HEADS):
        mixed = (weights[h][None] * pixels).reshape(pixel_rows.shape)
        high, low = split_two(mixed)
        flat_ref[h * size : (h + 1) * size, :] = dot(
            ev_ref[h * size : (h + 1) * size, :], jnp.concatenate([high, low, high], axis=0)
        )
    values = flat_ref[...].astype(bf16)
    merged = dot(values.T, out_w_ref[...])

    @pl.when(pl.program_id(0) < own_blocks)
    def _():
        values_ref[...] = values
        merged_ref[...] = merged

    unit_rows, _ = norm_parts(merged)
    normed = (unit_rows * gain_ref[...] + bias_ref[...]).astype(bf16)
    tall_s[...] = normed.T
    core, shard = place_ref[1], tall_s.shape[0] // (2 * n_z)
    for zz in range(n_z):
        at = slice(zz * shard, (zz + 1) * shard)
        keep_ref[at] = tall_s[pl.ds(pl.multiple_of((2 * zz + core) * shard, shard), shard), :]
        send_ref[at] = tall_s[pl.ds(pl.multiple_of((2 * zz + 1 - core) * shard, shard), shard), :]
    queries = dot(normed, wq_ref[...]).astype(bf16).astype(f32) * size ** (-0.5)
    keys = dot(normed, wk_ref[...])
    values = dot(normed, wv_ref[...])
    ones = jnp.where(lax.broadcasted_iota(jnp.int32, (keys.shape[0], size), 1) < 3, 1.0, 0.0)
    for h in range(q_ref.shape[0]):
        at = h * size
        q_ref[h] = queries[:, at : at + size].astype(bf16)
        key = keys[:, at : at + size]
        k_ref[h] = jnp.concatenate([key, key], axis=1).astype(bf16)
        v_ref[h] = jnp.concatenate([values[:, at : at + size], ones], axis=1).astype(bf16)


def attend_kernel(q_ref, k_ref, v_ref, out_ref, aug_ref):
    here, rows, size = q_ref.shape
    for h in range(here):
        aug_ref[h, :, : 2 * size] = jnp.concatenate(
            split_two(q_ref[h].astype(f32) * LOG2E), axis=1
        )

    def scores_of(h):
        return dot_nt(aug_ref[h, :, : 2 * size], k_ref[h])

    def finish(h, powers, top):
        mixed = dot(powers, v_ref[h])
        total = mixed[:, size : size + 1]
        lse = top + jnp.log(total) * LOG2E
        return (mixed[:, :size] / total).astype(bf16), columns(split_three(-lse), rows, 2 * size)

    done, waiting = [], None
    scores = scores_of(0)
    for h in range(here):
        later = scores_of(h + 1) if h + 1 < here else None
        top = jnp.max(scores, axis=-1, keepdims=True)
        powers = jnp.exp2(scores - top).astype(bf16)
        if waiting is not None:
            done.append(finish(*waiting))
        waiting = (h, powers, top)
        scores = later
    done.append(finish(*waiting))
    for h in range(here):
        aug_ref[h, :, 2 * size :] = done[h][1]
    out_ref[...] = jnp.concatenate([part for part, _ in done], axis=-1)


def attend_back_kernel(count, extra, *refs):
    extra_refs, refs = refs[:extra], refs[extra:]
    q_ref, k_ref, v_ref = refs[:3]
    aug_refs = refs[3 : 3 + count]
    out_refs = refs[3 + count : 3 + 2 * count]
    up_refs = refs[3 + 2 * count : 3 + 3 * count]
    full_ref = refs[3 + 3 * count]
    piece_refs = refs[4 + 3 * count : 4 + 4 * count]
    up_s, gq_ref, prob_s, slope_s = refs[4 + 4 * count :]
    step = pl.program_id(0)
    here, patches, size = q_ref.shape
    block = k_ref.shape[1]
    width = here * size
    mine = patches // count

    @pl.when(step == 0)
    def _():
        for h in range(here):
            at = h * size
            for d in range(count):
                upstream = up_refs[d][:, at : at + size]
                product = upstream.astype(f32) * out_refs[d][:, at : at + size].astype(f32)
                total = jnp.sum(product, axis=-1, keepdims=True)
                up_s[h, d * mine : (d + 1) * mine] = jnp.concatenate(
                    [upstream, columns(split_three(-total), mine, size)], axis=1
                )
            gq_ref[h] = jnp.zeros((size, patches), f32)

    chunk = min(256, mine)
    key_parts, value_parts = [], []
    ones = jnp.where(lax.broadcasted_iota(jnp.int32, (block, 2 * size), 1) < 3, 1.0, 0.0).astype(bf16)
    for h in range(here):
        keys, values = k_ref[h], v_ref[h]
        keys_wide = jnp.concatenate([keys, ones], axis=1)
        for at in range(0, patches, chunk):
            span = slice(at, at + chunk)
            rows = slice(at % mine, at % mine + chunk)
            probs = jnp.exp2(dot_nt(keys_wide, aug_refs[at // mine][h, rows]))
            prob_s[h, :, span] = probs.astype(bf16)
            slope_s[h, :, span] = (probs * dot_nt(values, up_s[h, span])).astype(bf16)
        value_parts.append(dot(prob_s[h], up_s[h])[:, :size])
        key_parts.append(dot(slope_s[h], q_ref[h]))
        gq_ref[h] += dot(keys.astype(f32).T[:size].astype(bf16), slope_s[h])
    rows = pl.ds(pl.multiple_of(step * block, block), block)
    full_ref[rows, width : 2 * width] = jnp.concatenate(key_parts, axis=-1).astype(bf16)
    full_ref[rows, 2 * width :] = jnp.concatenate(value_parts, axis=-1).astype(bf16)

    @pl.when(step == pl.num_programs(0) - 1)
    def _():
        scale = size ** (-0.5)
        query_parts = [gq_ref[h].T for h in range(here)]
        full_ref[:, :width] = (jnp.concatenate(query_parts, axis=-1) * scale).astype(bf16)
        for d in range(count):
            piece_refs[d][:, : 3 * width] = full_ref[d * mine : (d + 1) * mine, :]

    if extra:

        @pl.when(step == 0)
        def _():
            for d in range(count):
                piece_refs[d][:, 3 * width :] = extra_refs[d][...]


def mlp_kernel(pieces, count, *refs):
    place_ref = refs[0]
    att_refs = refs[1 : 1 + pieces]
    merged_ref, proj_ref, gain_ref, bias_ref, cot_ref, win_ref, wout_ref = refs[1 + pieces : 8 + pieces]
    outs = refs[8 + pieces :]
    (
        out_ref, att_t_ref, normed_t_ref, send_ref, keep_ref, ghid_ref, gstream_ref, glow_ref,
        gains_ref,
    ) = outs[:9]
    gatt_refs = outs[9 : 9 + count]
    att_s, normed_s, stream_s, unit_s, inv_s, out_s, gn_s, tall_s = outs[9 + count :]
    step = pl.program_id(0)
    me = place_ref[0]
    cols = gatt_refs[0].shape[1]

    @pl.when(step == 0)
    def _():
        if pieces == 1:
            attended = att_refs[0][...]
        else:
            for d in range(pieces):
                att_s[:, pl.ds(pl.multiple_of((me ^ d) * cols, cols), cols)] = att_refs[d][...]
            attended = att_s[...]
        att_t_ref[...] = attended.T
        stream = merged_ref[...] + dot(attended, proj_ref[...])
        unit_rows, inverse = norm_parts(stream)
        stream_s[...] = stream
        unit_s[...] = unit_rows
        inv_s[...] = inverse
        normed = (unit_rows * gain_ref[...] + bias_ref[...]).astype(bf16)
        normed_s[...] = normed
        normed_t_ref[...] = normed.T
        out_s[...] = jnp.zeros_like(out_s)
        gn_s[...] = jnp.zeros_like(gn_s)

    tile = ghid_ref.shape[1]
    sub = min(256, tile)
    spans = [slice(at, at + sub) for at in range(0, tile, sub)]
    normed_rows, upstream_rows = normed_s[...], cot_ref[...]

    def products(span):
        return dot(normed_rows, win_ref[:, span]), dot_nt(upstream_rows, wout_ref[span, :])

    def shape(hidden, g_active):
        below = 0.5 + 0.5 * lax.erf(hidden * (0.5**0.5))
        density = jnp.exp(-0.5 * hidden * hidden) * ((2.0 * jnp.pi) ** (-0.5))
        return (hidden * below).astype(bf16), (g_active * (below + hidden * density)).astype(bf16)

    actives, grads, sums = [], [], []

    def add(first, last):
        span = slice(spans[first].start, spans[last].stop)
        active = jnp.concatenate(actives[first : last + 1], axis=1)
        grad = jnp.concatenate(grads[first : last + 1], axis=1)
        sums.append((dot(active, wout_ref[span, :]), dot_nt(grad, win_ref[:, span])))

    ready = products(spans[0])
    for i, span in enumerate(spans):
        later = products(spans[i + 1]) if i + 1 < len(spans) else None
        if i == len(spans) // 2 + 1:
            add(0, len(spans) // 2 - 1)
        active, grad = shape(*ready)
        actives.append(active)
        grads.append(grad)
        ready = later
    add(len(spans) // 2 if sums else 0, len(spans) - 1)
    for span, active, grad in zip(spans, actives, grads):
        ghid_ref[:, span] = grad
        tall_s[span, :] = active.T
    half = tile // 2
    core = place_ref[1]
    send_ref[...] = tall_s[pl.ds(pl.multiple_of((1 - core) * half, half), half), :]
    keep_ref[...] = tall_s[pl.ds(pl.multiple_of(core * half, half), half), :]
    out_s[...] += sum(pair[0] for pair in sums)
    gn_s[...] += sum(pair[1] for pair in sums)

    @pl.when(step == pl.num_programs(0) - 1)
    def _():
        out_ref[...] = (stream_s[...] + out_s[...]).astype(bf16)
        upstream = gn_s[...].astype(bf16).astype(f32)
        unit_rows = unit_s[...]
        g_stream = cot_ref[...].astype(f32) + norm_back(
            upstream, unit_rows, inv_s[...], gain_ref[...]
        )
        gstream_ref[...] = g_stream
        low = g_stream.astype(bf16)
        glow_ref[...] = low
        for d in range(count):
            rows = pl.ds(pl.multiple_of((me ^ d) * cols, cols), cols)
            gatt_refs[d][...] = dot_nt(low, proj_ref[rows, :]).astype(bf16)
        gains_ref[0:1, :] = jnp.sum(upstream * unit_rows, axis=0, keepdims=True)
        gains_ref[1:2, :] = jnp.sum(upstream, axis=0, keepdims=True)


def send_kernel(place_ref, main_rows, main_cols, side_rows, side_cols, out_ref):
    last = pl.program_id(0) == pl.num_programs(0) - 1

    def product(rows_ref, cols_ref):
        tall = rows_ref[...].reshape(-1, rows_ref.shape[-1])
        return dot(tall, cols_ref[...]).astype(bf16)

    @pl.when(jnp.logical_not(last))
    def _():
        out_ref[...] = product(main_rows, main_cols)

    @pl.when(last)
    def _():
        out_ref[...] = product(side_rows, side_cols)


def keep_kernel(count, *refs):
    main_rows, main_cols, main_got, side_rows, side_cols, side_got = refs[1:7]
    outs = refs[7:]
    step = pl.program_id(0)

    def product(rows_ref, cols_ref, got_ref):
        tall = rows_ref[...].reshape(-1, rows_ref.shape[-1])
        return (dot(tall, cols_ref[...]) + got_ref[...].astype(f32)).astype(bf16)

    for d in range(count):

        @pl.when(step == d)
        def _():
            first, second = outs[d], outs[count + d]
            main = product(main_rows, main_cols, main_got)
            cut = first.shape[1]
            rest = main.shape[1] - cut
            first[...] = main[:, :cut]
            second[:, :rest] = main[:, cut:]
            second[:, rest:] = product(side_rows, side_cols, side_got)


def pair_kernel(count, channels, vars_here, late_rows, *refs):
    place_ref = refs[0]
    keep_ref, got_ref, n_keep_ref, n_got_ref, fields_ref = refs[1:6]
    outs = refs[6:]
    depth, mine = fields_ref.shape
    rows = late_rows
    span = outs[0].shape[1]
    slots = depth // TABLES
    n_blocks = n_keep_ref.shape[1] // span
    f_rows = (outs[0].shape[0] - rows - n_blocks * HEADS) // (mine // span)
    row = lax.broadcasted_iota(jnp.int32, (f_rows, depth), 0)
    col = lax.broadcasted_iota(jnp.int32, (f_rows, depth), 1)
    n_total = (n_keep_ref[...] + n_got_ref[...].astype(f32)).astype(bf16)
    for d in range(count):
        q = place_ref[0] ^ d

        def block(ref):
            if len(ref.shape) == 3:
                return ref[d, :rows].astype(f32)
            return ref[:rows, pl.ds(pl.multiple_of(q * span, span), span)].astype(f32)

        outs[d][:rows] = (block(keep_ref) + block(got_ref)).astype(bf16)
        want = (row % channels) * slots + q * vars_here + row // channels
        picks = jnp.where((want == col) & (row < channels * vars_here), 1.0, 0.0).astype(bf16)
        picked = dot(picks, fields_ref[...]).astype(bf16)
        at = rows
        for b in range(n_blocks):
            outs[d][at : at + HEADS] = n_total[:, b * span : (b + 1) * span]
            at += HEADS
        for b in range(mine // span):
            outs[d][at : at + f_rows] = picked[:, b * span : (b + 1) * span]
            at += f_rows


def z_pieces_kernel(count, shard, n_z, *refs):
    pieces, outs, fields_ref, total_s = refs[1 : 1 + count], refs[1 + count : -2], refs[-2], refs[-1]
    me, z_at = refs[0][0], refs[0][2]
    rows, span = total_s.shape
    f_rows = fields_ref.shape[0]
    mine = fields_ref.shape[1] // count
    total = pieces[0][:rows].astype(f32)
    for piece in pieces[1:]:
        total = total + piece[:rows].astype(f32)
    total_s[...] = total.astype(bf16)
    for d in range(n_z):
        start = pl.multiple_of((z_at ^ d) * shard, shard)
        outs[d][:shard] = total_s[pl.ds(start, shard), :]
        outs[d][shard:] = total_s[n_z * shard :, :]
    for d in range(count):
        blocks = [
            pieces[d][rows + b * f_rows : rows + (b + 1) * f_rows] for b in range(mine // span)
        ]
        at = pl.multiple_of((me ^ d) * mine, mine)
        fields_ref[:, pl.ds(at, mine)] = jnp.concatenate(blocks, axis=1).astype(f32)


def assemble_kernel(count, parts, size, halves, *refs):
    me = refs[0][0]
    blocks, outs = refs[1 : 1 + count + halves], refs[1 + count + halves :]
    in_ref, proj_ref, qkv_ref, out_ref = outs
    a = in_ref.shape[1] // count
    b = proj_ref.shape[1] // count
    width = proj_ref.shape[1]
    for d in range(count):
        if halves and d == count - 1:
            rows = jnp.concatenate([ref[...] for ref in blocks[d:]], axis=1)
        else:
            rows = blocks[d][...]
        rows = rows.astype(f32)
        q = me ^ d if halves else d

        def span(at, step):
            return pl.ds(pl.multiple_of(at, step) if halves else at, step)

        in_ref[:, span(q * a, a)] = rows[:, :a]
        proj_ref[:, span(q * b, b)] = rows[:, a : a + b]
        at = a + b
        for part in range(parts):
            for third in range(3):
                to = third * width + q * b + part * size
                qkv_ref[:, span(to, size)] = rows[:, at : at + size]
                at += size
        out_ref[q] = rows[:, at:]


def z_sum_kernel(count, *refs):
    pieces, (rows_ref, n_ref) = refs[:count], refs[count:]
    total = pieces[0][...].astype(f32)
    for piece in pieces[1:]:
        total = total + piece[...].astype(f32)
    rows, span = rows_ref.shape
    rows_ref[...] = total[:rows].astype(bf16)
    for b in range(n_ref.shape[1] // span):
        n_ref[:, b * span : (b + 1) * span] = total[rows + b * HEADS : rows + (b + 1) * HEADS]


def final_kernel(count, *refs):
    place_ref = refs[0]
    pieces = refs[1 : 1 + count]
    n_ref, tables_ref, spread_ref, keys_ref, value_ref, qk_ref = refs[1 + count : 7 + count]
    outg_ref, valg_ref, keyg_ref, queryg_ref, embedg_ref, varg_ref, gains_ref, m_s = refs[7 + count :]
    shard, depth = tables_ref.shape
    width = m_s.shape[1]
    for d in range(count):
        span = pieces[d].shape[1]
        at = 0 if count == 1 else pl.multiple_of((place_ref[0] ^ d) * span, span)
        outg_ref[:, pl.ds(at, span)] = pieces[d][:shard].astype(f32)
        m_s[:, pl.ds(at, span)] = pieces[d][shard:].astype(f32)
    m_low = m_s[:depth, :].astype(bf16)
    n_high, n_low = split_two(n_ref[:, :depth])
    tables = tables_ref[...]
    valg_ref[...] = dot(tables, m_low)
    g_qk = dot_nt(tables, n_high) + dot_nt(tables, n_low)
    qk_high, qk_low = split_two(g_qk)
    spread = spread_ref[...]
    keyg_ref[...] = dot(qk_high, spread) + dot(qk_low, spread)
    head_at = lax.broadcasted_iota(jnp.int32, (HEADS, width), 1) // (width // HEADS)
    same = head_at == lax.broadcasted_iota(jnp.int32, (HEADS, width), 0)
    ones = jnp.where(same, 1.0, 0.0).astype(bf16)
    n_wide = dot(n_high.astype(f32).T.astype(bf16), ones) + dot(n_low.astype(f32).T.astype(bf16), ones)
    queryg_ref[...] = jnp.sum(n_wide * keys_ref[...], axis=0, keepdims=True)
    qk = qk_ref[...]
    table_grad = split_three(
        dot_nt(m_low, value_ref[...])
        + dot_nt(n_high.astype(f32).T.astype(bf16), qk)
        + dot_nt(n_low.astype(f32).T.astype(bf16), qk)
    )
    slots = depth // TABLES
    vars_here = varg_ref.shape[0]
    for ref, first, each in ((embedg_ref, 0, TABLES - 1), (varg_ref, TABLES - 1, 1)):
        row = lax.broadcasted_iota(jnp.int32, (each * vars_here, depth), 0)
        col = lax.broadcasted_iota(jnp.int32, (each * vars_here, depth), 1)
        want = (first + row % each) * slots + place_ref[0] * vars_here + row // each
        picks = jnp.where(want == col, 1.0, 0.0).astype(bf16)
        ref[...] = sum(dot(picks, part) for part in table_grad)
    gains_ref[...] = m_s[depth : depth + 8, :]


def back_kernel(count, parts, n_z, *refs):
    place_ref = refs[0]
    piece_refs = refs[1 : 1 + count * parts]
    (
        qkv_ref, merged_ref, gain_ref, gs_ref, out_w_ref, pix_ref, shi_ref, slo_ref, sthi_ref,
        stlo_ref, real_ref, ev_ref, values_ref, gains_two_ref,
        fields_ref, send_ref, keep_ref, slope_s, packed_s, m_ref, n_ref, grad_s,
    ) = refs[1 + count * parts :]
    step = pl.program_id(0)
    slots = real_ref.shape[0]
    if count == 1:
        packed = piece_refs[0][...]
    else:
        span = piece_refs[0].shape[1] // 3
        for third in range(3):
            for part in range(parts):
                for d in range(count):
                    at = third * (count * parts) + (place_ref[0] ^ d) * parts + part
                    packed_s[:, pl.ds(pl.multiple_of(at * span, span), span)] = piece_refs[
                        part * count + d
                    ][:, third * span : (third + 1) * span]
        packed = packed_s[...]
    unit_rows, inverse = norm_parts(merged_ref[...])
    upstream = dot_nt(packed, qkv_ref[...]).astype(bf16).astype(f32)
    g_merged = gs_ref[...] + norm_back(upstream, unit_rows, inverse, gain_ref[...])
    low = g_merged.astype(bf16)
    depth = pix_ref.shape[0]

    @pl.when(step == 0)
    def _():
        m_ref[...] = jnp.zeros_like(m_ref)
        n_ref[...] = jnp.zeros_like(n_ref)
        grad_s[...] = jnp.zeros_like(grad_s)
        m_ref[depth + 2 : depth + 4, :] = gains_two_ref[...]

    grad_s[...] += dot(values_ref[...], low)
    m_ref[depth : depth + 1, :] += jnp.sum(upstream * unit_rows, axis=0, keepdims=True)
    m_ref[depth + 1 : depth + 2, :] += jnp.sum(upstream, axis=0, keepdims=True)
    g_values = dot_nt(low, out_w_ref[...]).astype(bf16)

    pixel_rows = pix_ref[...]
    probs = variable_probs(pixel_rows, shi_ref[...], slo_ref[...], real_ref[...], slots)
    weights = probs.astype(bf16).astype(f32)
    pixels = pixel_rows.astype(f32).reshape(TABLES, slots, -1)
    size = ev_ref.shape[2]
    g_fields = jnp.zeros(pixels.shape, f32)
    for h in range(HEADS):
        rows = g_values[:, h * size : (h + 1) * size]
        both = dot_nt(ev_ref[h], rows)
        table = (both[:depth] + both[depth:]).reshape(pixels.shape)
        g_weights = jnp.sum(pixels * table, axis=0)
        total = jnp.sum(g_weights * probs[h], axis=0, keepdims=True)
        slope_s[h * slots : (h + 1) * slots, :] = (probs[h] * (g_weights - total)).astype(bf16)
        g_fields += weights[h][None] * table
        mixed = (weights[h][None] * pixels).reshape(pixel_rows.shape)
        pair = dot(jnp.concatenate(split_two(mixed), axis=0), rows)
        m_ref[:depth, h * size : (h + 1) * size] += pair[:depth] + pair[depth:]
    slopes = slope_s[...]
    fields_ref[...] = (
        g_fields.reshape(pixel_rows.shape) + dot(sthi_ref[...], slopes) + dot(stlo_ref[...], slopes)
    ).astype(bf16)
    n_ref[...] += dot_nt(pixel_rows, slopes)

    @pl.when(step == pl.num_programs(0) - 1)
    def _():
        core = place_ref[1]
        shard = grad_s.shape[0] // (2 * n_z)
        for zz in range(n_z):
            at = slice(zz * shard, (zz + 1) * shard)
            keep_ref[at] = grad_s[pl.ds(pl.multiple_of((2 * zz + core) * shard, shard), shard), :]
            send_ref[at] = grad_s[
                pl.ds(pl.multiple_of((2 * zz + 1 - core) * shard, shard), shard), :
            ].astype(bf16)
        top = n_z * shard
        middle = top + m_ref.shape[0]
        tables = m_ref[...]
        keep_ref[top:middle] = tables
        send_ref[top:middle] = tables.astype(bf16)
        columns = lax.broadcasted_iota(jnp.int32, n_ref.shape, 1)
        same = columns % slots == lax.broadcasted_iota(jnp.int32, n_ref.shape, 0) % slots
        n_high, n_low = split_two(jnp.where(same, n_ref[...], 0.0))
        heads = (HEADS, n_ref.shape[1])
        picks = lax.broadcasted_iota(jnp.int32, heads, 1) // slots
        picks = jnp.where(picks == lax.broadcasted_iota(jnp.int32, heads, 0), 1.0, 0.0).astype(bf16)
        n_rows = dot_nt(picks, n_high) + dot_nt(picks, n_low)
        keep_ref[middle:] = jnp.zeros((HEADS, keep_ref.shape[1]), f32)
        keep_ref[middle:, :depth] = n_rows
        send_ref[middle:] = keep_ref[middle:].astype(bf16)


def per_device(
    n_var, n_z, fields, var_mask, embed_weight, var_embed, agg_query, agg_key, agg_value, agg_out,
    norm1_gain, norm1_bias, attn_qkv, attn_proj, norm2_gain, norm2_bias, mlp_in, mlp_out, cotangent,
):
    n_item = 2 * n_z
    width = agg_key.shape[0]
    size = width // HEADS
    scale = size ** (-0.5)
    hidden_width = mlp_in.shape[1]
    vars_here, channels, patches = fields.shape[1:]
    slot_count = var_mask.shape[1]
    slots = -(-slot_count // 16) * 16
    mine = patches // n_var
    here = HEADS // n_var
    cols = here * size
    shard = width // n_item
    me = lax.axis_index("var")
    core = lax.axis_index("core")
    z_at = lax.axis_index("z")
    item = z_at * 2 + core
    rel = me ^ jnp.arange(n_var)
    rel_z = z_at ^ jnp.arange(n_z)
    place = jnp.stack([me, core, z_at]).astype(jnp.int32)
    lanes_fit = cols % 128 == 0

    def send(array, other):
        return lax.ppermute(array, "var", [(i, i ^ other) for i in range(n_var)])

    def send_z(array, other):
        return lax.ppermute(array, "z", [(i, i ^ other) for i in range(n_z)])

    def swap_core(array):
        return lax.ppermute(array, "core", [(0, 1), (1, 0)])

    def canonical(by_distance):
        return jnp.take(jnp.stack(by_distance, axis=0), rel, axis=0)

    def call(kernel, grid, in_specs, out_specs, out_shape, scratch, estimate, name, *args):
        return pl.pallas_call(
            kernel,
            grid_spec=pltpu.PrefetchScalarGridSpec(
                num_scalar_prefetch=1,
                grid=grid,
                in_specs=in_specs,
                out_specs=out_specs,
                scratch_shapes=scratch,
            ),
            out_shape=out_shape,
            compiler_params=params(),
            cost_estimate=estimate,
            name=name,
        )(place, *args)

    depth = TABLES * slots
    pixel_part = jnp.concatenate([fields[0], jnp.ones((vars_here, 1, patches), bf16)], axis=1)
    table_part = jnp.concatenate([embed_weight, var_embed[:, None, :]], axis=1)
    piece = jnp.concatenate([pixel_part, table_part], axis=2).reshape(TABLES * vars_here, -1)
    pieces = [piece] + [send(piece, d) for d in range(1, n_var)]
    real = jnp.pad(var_mask[0], (0, slots - slot_count)).astype(f32)[:, None]
    prep_in = pieces + [agg_query[None], agg_key, agg_value]
    maps = [(HEADS * slots, depth)] * 2 + [(depth, HEADS * slots)] * 2
    prep_out = (
        [((depth, patches), bf16), ((depth, width), bf16)]
        + [(shape, bf16) for shape in maps]
        + [
            ((width, 3 * depth), bf16),
            ((HEADS, 2 * depth, size), bf16),
            ((depth, width), f32),
            ((width, HEADS), bf16),
            ((HEADS, width), bf16),
        ]
    )
    (
        pixels, tables, score_high, score_low, score_high_t, score_low_t, ev_front, ev_back,
        table_keys, query_keys, spread,
    ) = call(
        partial(prep_kernel, n_var, vars_here, patches),
        (1,),
        [whole(array.shape) for array in prep_in],
        [whole(shape) for shape, _ in prep_out],
        [jax.ShapeDtypeStruct(shape, kind) for shape, kind in prep_out],
        [pltpu.VMEM((depth, patches + width), bf16)],
        cost(8 * depth * width * width, 4 * width * width),
        "prep",
        *prep_in,
    )

    gain_one, bias_one = norm1_gain[None], norm1_bias[None]
    gain_two, bias_two = norm2_gain[None], norm2_bias[None]

    if lanes_fit:
        qkv_parts = [attn_qkv] * 3
        qkv_specs = [
            pl.BlockSpec((width, cols), lambda i, at, third=third: (0, third * n_var + at[0]))
            for third in range(3)
        ]
    else:
        qkv_mine = lax.dynamic_index_in_dim(
            attn_qkv.reshape(width, 3, n_var, cols), me, axis=2, keepdims=False
        )
        qkv_parts = [qkv_mine[:, third] for third in range(3)]
        qkv_specs = [whole((width, cols))] * 3

    block = min(512, mine)
    steps = patches // block
    own = mine // block
    heads_shape = jax.ShapeDtypeStruct((here, patches, size), bf16)
    heads_spec = pl.BlockSpec((here, block, size), lambda i, _: (0, i, 0))
    wide_shape = jax.ShapeDtypeStruct((here, patches, 2 * size), bf16)
    wide_spec = pl.BlockSpec((here, block, 2 * size), lambda i, _: (0, i, 0))
    agg_values_t, merged, normed_send, normed_keep, queries, keys, values = call(
        partial(front_kernel, own, n_z),
        (steps,),
        [
            pl.BlockSpec((depth, block), lambda i, _: (0, i)),
            whole(score_high.shape),
            whole(score_low.shape),
            whole(real.shape),
            whole(ev_front.shape),
            whole(agg_out.shape),
            whole(gain_one.shape),
            whole(bias_one.shape),
        ]
        + qkv_specs,
        [
            pl.BlockSpec((width, block), lambda i, _: (0, jnp.minimum(i, own - 1))),
            pl.BlockSpec((block, width), lambda i, _: (jnp.minimum(i, own - 1), 0)),
            pl.BlockSpec((width // 2, block), lambda i, _: (0, i)),
            pl.BlockSpec((width // 2, block), lambda i, _: (0, i)),
            heads_spec,
            wide_spec,
            wide_spec,
        ],
        [
            jax.ShapeDtypeStruct((width, mine), bf16),
            jax.ShapeDtypeStruct((mine, width), f32),
            jax.ShapeDtypeStruct((width // 2, patches), bf16),
            jax.ShapeDtypeStruct((width // 2, patches), bf16),
            heads_shape,
            wide_shape,
            wide_shape,
        ],
        [pltpu.VMEM((width, block), f32), pltpu.VMEM((width, block), bf16)],
        cost(2 * patches * width * (width + 3 * cols + 256), 16 * patches * width),
        "front",
        pixels, score_high, score_low, real, ev_front, agg_out, gain_one, bias_one, *qkv_parts,
    )

    def attend(distance):
        return pl.pallas_call(
            attend_kernel,
            grid=(1,),
            in_specs=[
                pl.BlockSpec((here, mine, size), lambda i: (0, distance, 0)),
                whole(keys.shape),
                whole(values.shape),
            ],
            out_specs=[whole((mine, cols)), whole((here, mine, 4 * size))],
            out_shape=[
                jax.ShapeDtypeStruct((mine, cols), bf16),
                jax.ShapeDtypeStruct((here, mine, 4 * size), bf16),
            ],
            compiler_params=params(),
            cost_estimate=cost(
                4 * mine * patches * here * 256, 4 * patches * cols * 2, mine * patches * here
            ),
            name=f"attend{distance}",
        )(queries, keys, values)

    attended_by, aug_by, arrived = [None] * n_var, [None] * n_var, [None] * n_var
    for distance in reversed(range(n_var)):
        attended_by[distance], aug_by[distance] = attend(distance)
        arrived[distance] = (
            send(attended_by[distance], distance) if distance else attended_by[distance]
        )
    if not lanes_fit:
        arrived = [canonical(arrived).transpose(1, 0, 2).reshape(mine, width)]

    cot = cotangent[0]
    tile = 2 * hidden_width // n_item
    row_f32 = jax.ShapeDtypeStruct((mine, width), f32)
    row_bf16 = jax.ShapeDtypeStruct((mine, width), bf16)
    row_spec = whole((mine, width))
    tall_spec = whole((width, mine))
    tall_bf16 = jax.ShapeDtypeStruct((width, mine), bf16)
    piece_spec = whole((mine, cols))
    (
        output, attended_t, normed_two_t, active_send, active_keep, g_hidden, g_stream, g_stream_low,
        gains_two,
        *g_attended,
    ) = call(
        partial(mlp_kernel, len(arrived), n_var),
        (hidden_width // tile,),
        [whole(piece.shape) for piece in arrived]
        + [
            row_spec,
            whole((width, width)),
            whole(gain_two.shape),
            whole(bias_two.shape),
            row_spec,
            pl.BlockSpec((width, tile), lambda i, _: (0, i)),
            pl.BlockSpec((tile, width), lambda i, _: (i, 0)),
        ],
        [
            row_spec,
            tall_spec,
            tall_spec,
            pl.BlockSpec((tile // 2, mine), lambda i, _: (i, 0)),
            pl.BlockSpec((tile // 2, mine), lambda i, _: (i, 0)),
            pl.BlockSpec((mine, tile), lambda i, _: (0, i)),
            row_spec,
            row_spec,
            whole((2, width)),
        ]
        + [piece_spec] * n_var,
        [
            row_bf16,
            tall_bf16,
            tall_bf16,
            jax.ShapeDtypeStruct((hidden_width // 2, mine), bf16),
            jax.ShapeDtypeStruct((hidden_width // 2, mine), bf16),
            jax.ShapeDtypeStruct((mine, hidden_width), bf16),
            row_f32,
            row_bf16,
            jax.ShapeDtypeStruct((2, width), f32),
        ]
        + [jax.ShapeDtypeStruct((mine, cols), bf16)] * n_var,
        [
            pltpu.VMEM((mine, width), bf16),
            pltpu.VMEM((mine, width), bf16),
            pltpu.VMEM((mine, width), f32),
            pltpu.VMEM((mine, width), f32),
            pltpu.VMEM((mine, 1), f32),
            pltpu.VMEM((mine, width), f32),
            pltpu.VMEM((mine, width), f32),
            pltpu.VMEM((tile, mine), bf16),
        ],
        cost(
            2 * mine * width * (4 * hidden_width + 2 * width),
            4 * width * hidden_width + 16 * mine * width,
        ),
        "mlp",
        *arrived, merged, attn_proj, gain_two, bias_two, cot, mlp_in, mlp_out,
    )
    g_heads = [g_attended[0]] + [send(g_attended[d], d) for d in range(1, n_var)]

    kept_rows = n_z * shard

    def pair_product(tall, grads):
        return dot(tall, grads).astype(bf16)

    def pair_own(tall, grads, got):
        return (dot(tall, grads) + got.astype(f32)).astype(bf16)

    def column_block(array, start=0, total=None):
        rows = array.shape[0]
        total = total or array.shape[1]
        span = total // n_var
        if span % 128 == 0:
            return array, pl.BlockSpec((rows, span), lambda j, at: (0, start // span + (at[0] ^ j)))
        cut = array[:, start : start + total]
        cut = jnp.take(cut.reshape(rows, n_var, span).transpose(1, 0, 2), rel, axis=0)
        return cut, pl.BlockSpec((None, rows, span), lambda j, at: (j, 0, 0))

    def pair_send_two(main, side):
        spec = pl.BlockSpec((n_z, None, shard, mine), lambda j, at: (0, 1 - at[1], 0, 0))
        tiles = hidden_width // width
        return call(
                send_kernel,
                (tiles + 1,),
                [
                    spec,
                    pl.BlockSpec((mine, width), lambda j, at: (0, jnp.minimum(j, tiles - 1))),
                    spec,
                    whole((mine, width)),
                ],
                pl.BlockSpec((kept_rows, width), lambda j, at: (0, j)),
                jax.ShapeDtypeStruct((kept_rows, hidden_width + width), bf16),
                [],
                cost(2 * kept_rows * mine * (hidden_width + width), 24 * kept_rows * width, share=2),
                "send",
                main[0].reshape(n_z, 2, shard, mine), main[1],
                side[0].reshape(n_z, 2, shard, mine), side[1],
            )

    def pair_keep(main, side, got):
        args, specs, start = [], [], 0
        for tall, grads in (main, side):
            args.append(tall.reshape(n_z, 2, shard, mine))
            specs.append(pl.BlockSpec((n_z, None, shard, mine), lambda j, at: (0, at[1], 0, 0)))
            for array, spec in (column_block(grads), column_block(got, start, grads.shape[1])):
                args.append(array)
                specs.append(spec)
            start += grads.shape[1]
        main_span, side_span = main[1].shape[1] // n_var, side[1].shape[1] // n_var
        first = 3 * main_span // 4
        spans = [first] * n_var + [main_span - first + side_span] * n_var
        outs = call(
            partial(keep_kernel, n_var),
            (n_var,),
            specs,
            [whole((kept_rows, span)) for span in spans],
            [jax.ShapeDtypeStruct((kept_rows, span), bf16) for span in spans],
            [],
            cost(
                2 * kept_rows * mine * (main_span + side_span) * n_var, 24 * kept_rows * main_span, share=2
            ),
            "keep",
            *args,
        )
        return outs[:n_var], outs[n_var:]

    def add_all(first, *others):
        total = first.astype(f32)
        for other in others:
            total = total + other.astype(f32)
        return total.astype(bf16)

    def exchange(pieces):
        return [pieces[0]] + [send(pieces[d], d) for d in range(1, n_var)]


    main, side = (normed_two_t, g_hidden), (attended_t, g_stream_low)
    sent = pair_send_two(main, side)
    sent, g_heads, active_send = lax.optimization_barrier((sent, g_heads, active_send))
    got = swap_core(sent)
    got_mlp_out = swap_core(pair_product(active_send, cot))
    first, second = pair_keep(main, side, got)
    active_keep, first, second = lax.optimization_barrier((active_keep, first, second))
    first = exchange(first)
    g_mlp_out = pair_own(active_keep, cot, got_mlp_out)
    mlp_out_rows = lax.psum_scatter(g_mlp_out, "z", scatter_dimension=0, tiled=True)
    g_heads, _ = lax.optimization_barrier((g_heads, g_mlp_out))

    group = min(2, here)
    parts = here // group
    gcols = group * size
    back_block = min(1024, patches)

    def attend_back(part, queries, extra):
        group_spec = pl.BlockSpec((group, back_block, 2 * size), lambda i: (part, i, 0))
        side_spec = pl.BlockSpec((mine, gcols), lambda i: (0, part))
        piece_cols = 3 * gcols + sum(array.shape[1] for array in extra[:1])
        full, *pieces = pl.pallas_call(
            partial(attend_back_kernel, n_var, len(extra)),
            grid=(patches // back_block,),
            in_specs=[whole(array.shape) for array in extra]
            + [
                pl.BlockSpec((group, patches, size), lambda i: (part, 0, 0)),
                group_spec,
                group_spec,
            ]
            + [pl.BlockSpec((group, mine, 4 * size), lambda i: (part, 0, 0))] * n_var
            + [side_spec] * (2 * n_var),
            out_specs=[whole((patches, 3 * gcols))] + [whole((mine, piece_cols))] * n_var,
            out_shape=[jax.ShapeDtypeStruct((patches, 3 * gcols), bf16)]
            + [jax.ShapeDtypeStruct((mine, piece_cols), bf16)] * n_var,
            scratch_shapes=[
                pltpu.VMEM((group, patches, 2 * size), bf16),
                pltpu.VMEM((group, size, patches), f32),
                pltpu.VMEM((group, back_block, patches), bf16),
                pltpu.VMEM((group, back_block, patches), bf16),
            ],
            compiler_params=params(),
            cost_estimate=cost(
                10 * patches * patches * group * 256, 8 * patches * gcols * 2, patches * patches * group
            ),
            name=f"attend_back{part}",
        )(*extra, queries, keys, values, *aug_by, *attended_by, *g_heads)
        return full, pieces

    ride = kept_rows == mine and parts > 1
    g_qkv, packed_pieces = [], []
    for part in range(parts):
        full, pieces = attend_back(part, queries, second if ride and part == 0 else [])
        if part == 0:
            full, first = lax.optimization_barrier((full, first))
            first_sum = add_all(*first)
        if part < parts - 1:
            product = pair_product(normed_send, full)
            queries, first_sum, product = lax.optimization_barrier((queries, first_sum, product))
            g_qkv.append((full, product))
        if part == parts - 1:
            pieces, packed_pieces = lax.optimization_barrier((pieces, packed_pieces))
        packed_pieces += exchange(pieces)
    if ride:
        second = [piece[:, 3 * gcols :] for piece in packed_pieces[:n_var]]
    else:
        second = exchange(second)
    g_qkv.append((full, pair_product(normed_send, full)))
    second_sum = add_all(*second)
    columns = [first_sum, second_sum]
    columns += [pair_own(normed_keep, full, swap_core(product)) for full, product in g_qkv]
    both_sum = jnp.concatenate(columns, axis=1)
    def my_slice(array, axis):
        return lax.dynamic_slice_in_dim(array, item * shard, shard, axis=axis)

    final_in = [my_slice(tables, 1).T, spread, table_keys, my_slice(agg_value, 0), my_slice(query_keys, 0)]
    packed_pieces, both_sum, final_in = lax.optimization_barrier((packed_pieces, both_sum, final_in))
    both_rows = lax.psum_scatter(both_sum, "z", scatter_dimension=0, tiled=True)
    count = n_var
    if not lanes_fit:
        packed = [
            canonical(packed_pieces[part * n_var : (part + 1) * n_var]) for part in range(parts)
        ]
        packed = jnp.stack(packed, axis=0).reshape(parts, n_var, mine, 3, gcols)
        packed_pieces = [packed.transpose(2, 3, 1, 0, 4).reshape(mine, 3 * width)]
        count, parts = 1, 1
    packed_cols = 3 * gcols if lanes_fit else 3 * width

    row_block = pl.BlockSpec((block, width), lambda i, _: (i, 0))
    table_rows = -(-(depth + 4) // 16) * 16
    late_rows = kept_rows + table_rows
    g_fields, late_send, late_keep = call(
        partial(back_kernel, count, parts, n_z),
        (own,),
        [pl.BlockSpec((block, packed_cols), lambda i, _: (i, 0)) for piece in packed_pieces]
        + [
            whole(attn_qkv.shape),
            row_block,
            whole(gain_one.shape),
            row_block,
            whole(agg_out.shape),
            pl.BlockSpec((depth, block), lambda i, _: (0, i)),
            whole(score_high.shape),
            whole(score_low.shape),
            whole((depth, HEADS * slots)),
            whole((depth, HEADS * slots)),
            whole(real.shape),
            whole(ev_back.shape),
            pl.BlockSpec((width, block), lambda i, _: (0, i)),
            whole((2, width)),
        ],
        [
            pl.BlockSpec((depth, block), lambda i, _: (0, i)),
            whole((late_rows + HEADS, width)),
            whole((late_rows + HEADS, width)),
        ],
        [
            jax.ShapeDtypeStruct((depth, mine), bf16),
            jax.ShapeDtypeStruct((late_rows + HEADS, width), bf16),
            jax.ShapeDtypeStruct((late_rows + HEADS, width), f32),
        ],
        [
            pltpu.VMEM((HEADS * slots, block), bf16),
            pltpu.VMEM((block, 3 * width), bf16),
            pltpu.VMEM((table_rows, width), f32),
            pltpu.VMEM((depth, HEADS * slots), f32),
            pltpu.VMEM((width, width), f32),
        ],
        cost(2 * mine * width * 4 * width, 8 * width * width + 20 * mine * width),
        "back",
        *packed_pieces, attn_qkv, merged, gain_one, g_stream, agg_out, pixels, score_high, score_low,
        score_high_t, score_low_t, real, ev_back, agg_values_t, gains_two,
    )

    late_send, mlp_out_rows = lax.optimization_barrier((late_send, mlp_out_rows))
    out_block = mlp_out_rows.shape[0] // n_var
    mlp_out_by = exchange(
        [
            lax.dynamic_slice_in_dim(mlp_out_rows, (me ^ d) * out_block, out_block, axis=0)
            for d in range(n_var)
        ]
    )
    mlp_out_rows = add_all(*mlp_out_by).reshape(shard, -1)

    late_got = swap_core(late_send)
    late_span = width // n_var
    n_blocks = -(-depth // late_span)
    n_spec = pl.BlockSpec((HEADS, n_blocks * late_span), lambda j, at: (late_rows // HEADS, 0))
    sum_rows = late_rows + n_blocks * HEADS
    f_rows = -(-channels * vars_here // 16) * 16
    piece_rows = sum_rows + f_rows * (mine // late_span)
    late_args = [late_keep, late_got]
    if late_span % 128:
        late_args = [
            jnp.take(array.reshape(-1, n_var, late_span).transpose(1, 0, 2), rel, axis=0)
            for array in late_args
        ]
    late_pieces = call(
        partial(pair_kernel, n_var, channels, vars_here, late_rows),
        (1,),
        [whole(array.shape) for array in late_args] + [n_spec, n_spec, whole((depth, mine))],
        [whole((piece_rows, late_span))] * n_var,
        [jax.ShapeDtypeStruct((piece_rows, late_span), bf16)] * n_var,
        [],
        cost(piece_rows * width, 8 * piece_rows * width),
        "late_pair",
        *late_args, late_keep, late_got, g_fields,
    )
    late_pieces = exchange(late_pieces)
    late_pieces, both_rows = lax.optimization_barrier((late_pieces, both_rows))
    rows_all = jnp.concatenate([both_rows, mlp_out_rows], axis=1)
    halves = 1 if n_var == 4 and lanes_fit else 0
    if halves:
        near = [send(rows_all, 1), send(rows_all, 2)]
    else:
        rows_all = list(lax.all_gather(rows_all, "var", axis=0))
    z_rows = shard + table_rows + n_blocks * HEADS
    *z_pieces, fields_grad = call(
        partial(z_pieces_kernel, n_var, shard, n_z),
        (1,),
        [whole((piece_rows, late_span))] * n_var,
        [whole((z_rows, late_span))] * n_z + [whole((f_rows, patches))],
        [jax.ShapeDtypeStruct((z_rows, late_span), bf16)] * n_z
        + [jax.ShapeDtypeStruct((f_rows, patches), f32)],
        [pltpu.VMEM((sum_rows, late_span), bf16)],
        cost(piece_rows * width, 2 * piece_rows * width),
        "late_z",
        *late_pieces,
    )
    z_pieces = [z_pieces[0]] + [send_z(z_pieces[d], d) for d in range(1, n_z)]
    late_rows_mine, n_all = pl.pallas_call(
        partial(z_sum_kernel, n_z),
        out_shape=[
            jax.ShapeDtypeStruct((shard + table_rows, late_span), bf16),
            jax.ShapeDtypeStruct((HEADS, n_blocks * late_span), f32),
        ],
        compiler_params=params(),
        cost_estimate=cost(z_rows * width, 2 * z_rows * width),
        name="late_sum",
    )(*z_pieces)

    fields_grad = fields_grad[: channels * vars_here].reshape(1, vars_here, channels, patches)
    if halves:
        late_rows_mine, near = lax.optimization_barrier((late_rows_mine, near))
        half = rows_all.shape[1] // 2
        rows_all = [rows_all] + near + [send(near[0][:, :half], 2), send(near[1][:, half:], 1)]
    late_by = exchange([late_rows_mine] * n_var)
    if late_span % 128:
        late_by = [canonical(late_by).transpose(1, 0, 2).reshape(shard + table_rows, width)]
    small_shapes = [(1, width), (channels * vars_here, shard), (vars_here, shard), (8, width)]
    final_in = [n_all] + final_in
    agg_out_grad, agg_value_grad, agg_key_grad, query_row, embed_weight_grad, var_embed_grad, gains = call(
        partial(final_kernel, len(late_by)),
        (1,),
        [whole(array.shape) for array in late_by + final_in],
        [whole((shard, width))] * 3
        + [whole(shape) for shape in small_shapes],
        [jax.ShapeDtypeStruct((shard, width), f32)] * 3
        + [jax.ShapeDtypeStruct(shape, f32) for shape in small_shapes],
        [pltpu.VMEM((table_rows, width), f32)],
        cost(2 * shard * width * 3 * depth, 12 * shard * width),
        "final",
        *late_by, *final_in,
    )
    gains = my_slice(gains, 1)
    agg_query_grad = my_slice(query_row[0], 0) * scale
    embed_weight_grad = embed_weight_grad.reshape(vars_here, channels, shard)

    row_shapes = [
        jax.ShapeDtypeStruct((shard, hidden_width), f32),
        jax.ShapeDtypeStruct((shard, width), f32),
        jax.ShapeDtypeStruct((shard, 3 * width), f32),
        jax.ShapeDtypeStruct((n_var, shard, out_block * width // shard), f32),
    ]
    mlp_in_grad, attn_proj_grad, attn_qkv_grad, mlp_out_grad = call(
        partial(assemble_kernel, n_var, here // group, gcols, halves),
        (1,),
        [whole(array.shape) for array in rows_all],
        [whole(row.shape) for row in row_shapes],
        row_shapes,
        [],
        cost(shard * 9 * width, 6 * shard * 9 * width),
        "assemble",
        *rows_all,
    )
    mlp_out_grad = mlp_out_grad.reshape(n_var * out_block, width)
    return (
        output[None],
        fields_grad,
        embed_weight_grad,
        var_embed_grad,
        agg_query_grad,
        agg_key_grad,
        agg_value_grad,
        agg_out_grad,
        gains[0],
        gains[1],
        attn_qkv_grad,
        attn_proj_grad,
        gains[2],
        gains[3],
        mlp_in_grad,
        mlp_out_grad,
    )


def solution(mesh):
    n_var, n_item = mesh.shape["var"], mesh.shape["item"]
    items = ("z", "core")
    return jax.shard_map(
        partial(per_device, n_var, n_item // 2),
        mesh=Mesh(mesh.devices.reshape(n_var, n_item // 2, 2), ("var", "z", "core")),
        in_specs=(
            P(items, "var", None, None),
            P(items, None),
            P("var", None, None),
            P("var", None),
            P(),
            P(),
            P(),
            P(),
            P(),
            P(),
            P(),
            P(),
            P(),
            P(),
            P(),
            P(),
            P(items, "var", None),
        ),
        out_specs=(
            P(items, "var", None),
            P(items, "var", None, None),
            P("var", None, items),
            P("var", items),
            P(items),
            P(items, None),
            P(items, None),
            P(items, None),
            P(items),
            P(items),
            P(items, None),
            P(items, None),
            P(items),
            P(items),
            P(items, None),
            P(items, None),
        ),
        check_vma=False,
    )
```

time: 1380 us -> 368 us (0.27)
  matrix products: 475 us -> 15.6 us
  waiting for transfers between devices: 455 us -> 48.2 us
  Pallas kernels: 0 us -> 212 us
  blocking collectives: 177 us -> 0 us
  local copies, waits for them, and re-layouts: 153 us -> 15.5 us
  other arithmetic: 87.1 us -> 12.7 us
  starting transfers between devices: 8.87 us -> 43.6 us
    dot_general x34 -> x6, matrix products: 447 us -> 15.6 us  [dot(): lax.dot_general(a, b, (((1,), (0,)), ((), ())), preferred_element_type=f32)]
    pallas_call x0 -> x17, Pallas kernels: none -> 212 us  [the longest x10 117 us: call(): pl.pallas_call(kernel, grid_spec=pltpu.PrefetchScalarGridSpec(num_scalar_...]
    all_to_all x1 -> x0, waiting for transfers between devices: 174 us -> none  [per_device(): lax.all_to_all(tokens_var, 'var', split_axis=2, concat_axis=1, tiled=True)]
    all_to_all x1 -> x0, blocking collectives: 141 us -> none  [per_device(): lax.all_to_all(g_tokens, 'var', split_axis=1, concat_axis=2, tiled=True)]
    psum x1 -> x0, waiting for transfers between devices: 102 us -> none  [per_device(): lax.psum(r_key.astype(jnp.bfloat16), 'var').astype(jnp.float32)]
    reduce_scatter x8 -> x2, waiting for transfers between devices: 107 us -> 6.66 us  [the longest x1 6.65 us: per_device(): both_rows = lax.psum_scatter(both_sum, 'z', scatter_dimension=0, tiled=True)]
    all_gather x2 -> x0, waiting for transfers between devices: 70.8 us -> none  [the longest x1 50.8 us: per_device(): lax.all_gather(keys_local, 'var', axis=1, tiled=True)]
    convert_element_type x19 -> x4, other arithmetic: 74.7 us -> 6.57 us  [the longest x1 3.6 us: pair_own(): return (dot(tall, grads) + got.astype(f32)).astype(bf16)]
  transfers between devices with their start and end apart: 15 -> 41, of which waited for: 7 -> 17; matrix products, arithmetic and copies ran while one was open for 25% -> 9% of each run, Pallas kernels for 0% -> 30%
where the time goes in v1:
time: 368 us; the launch traced here: 362 us
  Pallas kernels  212 us (58%)
  waiting for transfers between devices  48.2 us (13%)
  starting transfers between devices  43.6 us (12%)
  matrix products  15.6 us (4%)
  local copies, waits for them, and re-layouts  15.5 us (4%)
  between operations  14.7 us (4%)
  other arithmetic  12.7 us (3%)
    pallas_call x10, Pallas kernels, call(): pl.pallas_call(kernel, grid_spec=pltpu.PrefetchScalarGridSpec(num_scalar_...  117 us
    pallas_call x2, Pallas kernels, attend_back(): pl.pallas_call(partial(attend_back_kernel, n_var, len(extra)), grid=(patc...  58 us
    ppermute x31, starting transfers between devices, send(): return lax.ppermute(array, 'var', [(i, i ^ other) for i in range(n_var)])  37.9 us
    pallas_call x4, Pallas kernels, attend(): pl.pallas_call(attend_kernel, grid=(1,), in_specs=[pl.BlockSpec((here, mi...  35.3 us
    ppermute x31, waiting for transfers between devices, send(): return lax.ppermute(array, 'var', [(i, i ^ other) for i in range(n_var)])  28.6 us
    dot_general x6, matrix products, dot(): lax.dot_general(a, b, (((1,), (0,)), ((), ())), preferred_element_type=f32)  15.6 us
    ppermute x3, waiting for transfers between devices, send_z(): return lax.ppermute(array, 'z', [(i, i ^ other) for i in range(n_z)])  8.8 us
  transfers between devices with their start and end apart: 41, of which 17 were waited for; matrix products, arithmetic and copies ran while one was open for 9% of the time, Pallas kernels for 30%

profile of v1, /device:TPU:0, one launch (start us, length us, event | category | flops | bytes accessed | tf_op | source)
XLA Modules:
  0.0 362.0 jit_solution(9330915972548634338)
XLA Ops:
  8.8 3.0 collective-permute-start
  19.5 7.1 %prep.1 = (bf16[80,2048]{1,0:T(8,128)(2,1)}, bf16[80,1024]{1,0:T(8,128)(2,1)}, bf16[256,80]{1,0:T(8,128)(2,1)}, bf16[256,80]{1,0:T(8,128)(2,1)}, bf16[80,256]{1,...) custom-call(s32[3]{0:T(128)} %pad_add_fusion.refs_0_.place_ref, ...), custom_call_target="tpu_custom_call" | custom-call | flops 33554432 | bytes 209715 | tf_op jit(solution)/shard_map/prep/pallas_call | solution.py:685
  26.6 23.5 %front.1 = (bf16[1024,512]{1,0:T(8,128)(2,1)}, f32[512,1024]{1,0:T(8,128)}, bf16[512,2048]{1,0:T(8,128)(2,1)}, bf16[512,2048]{1,0:T(8,128)(2,1)}, bf16[4,2048,64...) custom-call(s32[3]{0:T(128)} %pad_add_fusion.refs_0_.place_ref, ...), custom_call_target="tpu_custom_call" | custom-call | flops 429496736 | bytes 1677721 | tf_op jit(solution)/shard_map/front/pallas_call | solution.py:685
  50.1 8.8 %attend1.1 = (bf16[512,256]{1,0:T(8,128)(2,1)}, bf16[4,512,256]{2,1,0:T(8,128)(2,1)}) custom-call(bf16[4,2048,64]{2,1,0:T(8,128)(2,1)} %get-tuple-element.218.q_ref.refs_4_.refs_0_, bf16[4,2048,128]{2,1,0:T(8,128)(2,1)} %get-tuple-element.162.k_ref.refs_5_.refs_1_, bf16[4,2048,128]{2,1,0:T(8,128)(2,1)} %get-tuple-element.163.v_ref.refs_6_.refs_2_), custom_call_target="tpu_custom_call" | custom-call | flops 214748368 | bytes 209715 | tf_op jit(solution)/shard_map/attend1/pallas_call | solution.py:796
  58.9 8.8 %attend2.1 = (bf16[512,256]{1,0:T(8,128)(2,1)}, bf16[4,512,256]{2,1,0:T(8,128)(2,1)}) custom-call(bf16[4,2048,64]{2,1,0:T(8,128)(2,1)} %get-tuple-element.218.q_ref.refs_4_.refs_0_, bf16[4,2048,128]{2,1,0:T(8,128)(2,1)} %get-tuple-element.162.k_ref.refs_5_.refs_1_, bf16[4,2048,128]{2,1,0:T(8,128)(2,1)} %get-tuple-element.163.v_ref.refs_6_.refs_2_), custom_call_target="tpu_custom_call" | custom-call | flops 214748368 | bytes 209715 | tf_op jit(solution)/shard_map/attend2/pallas_call | solution.py:796
  67.7 9.0 %attend3.1 = (bf16[512,256]{1,0:T(8,128)(2,1)}, bf16[4,512,256]{2,1,0:T(8,128)(2,1)}) custom-call(bf16[4,2048,64]{2,1,0:T(8,128)(2,1)} %get-tuple-element.218.q_ref.refs_4_.refs_0_, bf16[4,2048,128]{2,1,0:T(8,128)(2,1)} %get-tuple-element.162.k_ref.refs_5_.refs_1_, bf16[4,2048,128]{2,1,0:T(8,128)(2,1)} %get-tuple-element.163.v_ref.refs_6_.refs_2_), custom_call_target="tpu_custom_call" | custom-call | flops 214748368 | bytes 209715 | tf_op jit(solution)/shard_map/attend3/pallas_call | solution.py:796
  80.2 8.8 %attend0.1 = (bf16[512,256]{1,0:T(8,128)(2,1)}, bf16[4,512,256]{2,1,0:T(8,128)(2,1)}) custom-call(bf16[4,2048,64]{2,1,0:T(8,128)(2,1)} %get-tuple-element.218.q_ref.refs_4_.refs_0_, bf16[4,2048,128]{2,1,0:T(8,128)(2,1)} %get-tuple-element.162.k_ref.refs_5_.refs_1_, bf16[4,2048,128]{2,1,0:T(8,128)(2,1)} %get-tuple-element.163.v_ref.refs_6_.refs_2_), custom_call_target="tpu_custom_call" | custom-call | flops 214748368 | bytes 209715 | tf_op jit(solution)/shard_map/attend0/pallas_call | solution.py:796
  90.8 32.2 %mlp.1 = (bf16[512,1024]{1,0:T(8,128)(2,1)}, bf16[1024,512]{1,0:T(8,128)(2,1)}, bf16[1024,512]{1,0:T(8,128)(2,1)}, bf16[2048,512]{1,0:T(8,128)(2,1)}, bf16[2048,...) custom-call(s32[3]{0:T(128)} %pad_add_fusion.refs_0_.place_ref, ...), custom_call_target="tpu_custom_call" | custom-call | flops 966367616 | bytes 1258291 | tf_op jit(solution)/shard_map/mlp/pallas_call | solution.py:685
  126.5 8.6 %send.1 = bf16[512,5120]{1,0:T(8,128)(2,1)} custom-call(s32[3]{0:T(128)} %pad_add_fusion.refs_0_.place_ref, bf16[4,2,128,512]{3,2,1,0:T(8,128)(2,1)} %bitcast.57, bf16[512,4096]{1,0:T(8,128)(2,1)} %get-tuple-element.172.main_cols.refs_2_, bf16[4,2,128,512]{3,2,1,0:T(8,128)(2,1)} %bitcast.55, bf16[512,1024]{1,0:T(8,128)(2,1)} %get-tuple-element.174.side_cols.refs_5_), custom_call_target="tpu_custom_call" | custom-call | flops 5368709120 | bytes 25165824 | tf_op jit(solution)/shard_map/send/pallas_call | solution.py:685
  135.4 4.3 %convolution_convert_fusion = bf16[2048,1024]{1,0:T(8,128)(2,1)} fusion(bf16[2048,512]{1,0:T(8,128)(2,1)S(1)} %copy-done.34, bf16[1,512,1024]{2,1,0:T(8,128)(2,1)S(1)} %copy-done.13), kind=kOutput, calls=%fused_computation.1 | convolution fusion | flops 2149580800 | bytes 7340032 | tf_op jit(solution)/shard_map/dot_general | solution.py:25
  140.3 4.1 %collective-permute-done.9.refs_3_.refs_6_ = bf16[512,5120]{1,0:T(8,128)(2,1)} collective-permute-done((bf16[512,5120]{1,0:T(8,128)(2,1)}, bf16[512,5120]{1,0:T(8,128)(2,1)}, u32[]{:S(2)}, u32[]{:S(2)}) %collective-permute-start.9) | collective-permute-done | bytes 5242912 | tf_op jit(solution)/shard_map/ppermute | solution.py:679
  144.4 10.1 %keep.1 = (bf16[512,768]{1,0:T(8,128)(2,1)}, bf16[512,768]{1,0:T(8,128)(2,1)}, bf16[512,768]{1,0:T(8,128)(2,1)}, bf16[512,768]{1,0:T(8,128)(2,1)}, bf16[512,512]...) custom-call(s32[3]{0:T(128)} %pad_add_fusion.refs_0_.place_ref, ...), custom_call_target="tpu_custom_call" | custom-call | flops 5368709120 | bytes 25165824 | tf_op jit(solution)/shard_map/keep/pallas_call | solution.py:685
  154.5 3.9 %fusion.7 = f32[2048,1024]{1,0:T(8,128)S(1)} fusion(bf16[2048,512]{1,0:T(8,128)(2,1)} %get-tuple-element.201, bf16[1,512,1024]{2,1,0:T(8,128)(2,1)S(1)} %copy-done.13), kind=kOutput, calls=%fused_computation.33 | convolution fusion | flops 2147483648 | bytes 11534336 | tf_op jit(solution)/shard_map/dot_general | solution.py:25
  158.4 3.6 add_convert_fusion
  168.1 30.0 %attend_back0.1 = (bf16[2048,384]{1,0:T(8,128)(2,1)}, bf16[512,896]{1,0:T(8,128)(2,1)}, bf16[512,896]{1,0:T(8,128)(2,1)}, bf16[512,896]{1,0:T(8,128)(2,1)}, bf16[512,896]{1,0:T(8,128)(2,1)}) custom-call(bf16[512,512]{1,0:T(8,128)(2,1)} %get-tuple-element.189.refs_0_, bf16[512,512]{1,0:T(8,128)(2,1)} %get-tuple-element.190.refs_1_, ...), custom_call_target="tpu_custom_call" | custom-call | flops 1073741824 | bytes 209715 | tf_op jit(solution)/shard_map/attend_back0/pallas_call | solution.py:990
  203.3 2.0 convolution_convert_fusion.2
  205.3 28.0 %attend_back1.1 = (bf16[2048,384]{1,0:T(8,128)(2,1)}, bf16[512,384]{1,0:T(8,128)(2,1)}, bf16[512,384]{1,0:T(8,128)(2,1)}, bf16[512,384]{1,0:T(8,128)(2,1)}, bf16[512,384]{1,0:T(8,128)(2,1)}) custom-call(bf16[4,2048,64]{2,1,0:T(8,128)(2,1)} %get-tuple-element.218.q_ref.refs_4_.refs_0_, bf16[4,2048,128]{2,1,0:T(8,128)(2,1)} %get-tuple-element.162.k_ref.refs_5_.refs_1_, ...), custom_call_target="tpu_custom_call" | custom-call | flops 1073741824 | bytes 209715 | tf_op jit(solution)/shard_map/attend_back1/pallas_call | solution.py:990
  233.3 2.8 convolution_convert_fusion.1
  238.1 2.8 collective-permute-done.15.refs_3_
  249.0 4.2 %collective-permute-done.17.refs_6_ = bf16[512,384]{1,0:T(8,128)(2,1)S(1)} collective-permute-done((bf16[512,384]{1,0:T(8,128)(2,1)}, bf16[512,384]{1,0:T(8,128)(2,1)S(1)}, u32[]{:S(2)}, u32[]{:S(2)}) %collective-permute-start.17) | collective-permute-done | bytes 393248 | tf_op jit(solution)/shard_map/ppermute | solution.py:673
  253.7 5.7 %collective-permute-done.19.refs_8_ = bf16[512,384]{1,0:T(8,128)(2,1)} collective-permute-done((bf16[512,384]{1,0:T(8,128)(2,1)}, bf16[512,384]{1,0:T(8,128)(2,1)}, u32[]{:S(2)}, u32[]{:S(2)}) %collective-permute-start.19) | collective-permute-done | bytes 393248 | tf_op jit(solution)/shard_map/ppermute | solution.py:673
  259.4 18.8 %back.1 = (bf16[80,512]{1,0:T(8,128)(2,1)}, bf16[624,1024]{1,0:T(8,128)(2,1)}, f32[624,1024]{1,0:T(8,128)}) custom-call(s32[3]{0:T(128)} %pad_add_fusion.refs_0_.place_ref, bf16[512,896]{1,0:T(8,128)(2,1)} %get-tuple-element.243.refs_1_, bf16[512,896]{1,0:T(8,128)(2,1)} %copy-done.3, bf16[512,896]{1,0:T(8,128)(2,1)} %copy-done.4, ...), custom_call_target="tpu_custom_call" | custom-call | flops 214748368 | bytes 943718 | tf_op jit(solution)/shard_map/back/pallas_call | solution.py:685
  284.3 4.1 %late_pair.1 = (bf16[656,256]{1,0:T(8,128)(2,1)}, bf16[656,256]{1,0:T(8,128)(2,1)}, bf16[656,256]{1,0:T(8,128)(2,1)}, bf16[656,256]{1,0:T(8,128)(2,1)}) custom-call(s32[3]{0:T(128)} %pad_add_fusion.refs_0_.place_ref, f32[624,1024]{1,0:T(8,128)} %get-tuple-element.257.refs_1_.refs_3_, bf16[624,1024]{1,0:T(8,128)(2,1)} %copy-done, ...), custom_call_target="tpu_custom_call" | custom-call | flops 33587 | bytes 268697 | tf_op jit(solution)/shard_map/late_pair/pallas_call | solution.py:685
  291.9 3.1 collective-permute-done.30
  297.0 6.6 %reduce-scatter.5.cloned.1.call-done = bf16[128,2048]{1,0:T(8,128)(2,1)} async-done(((bf16[512,2048]{1,0:T(8,128)(2,1)}), bf16[128,2048]{1,0:T(8,128)(2,1)}) %reduce-scatter.5.cloned.1.call-update) | async-done | bytes 524304 | tf_op jit(solution)/shard_map/reduce_scatter | solution.py:1046
  303.6 5.7 %collective-permute-done.25.refs_4_ = bf16[656,256]{1,0:T(8,128)(2,1)S(1)} collective-permute-done((bf16[656,256]{1,0:T(8,128)(2,1)}, bf16[656,256]{1,0:T(8,128)(2,1)S(1)}, u32[]{:S(2)}, u32[]{:S(2)}) %collective-permute-start.25) | collective-permute-done | bytes 335904 | tf_op jit(solution)/shard_map/ppermute | solution.py:673
  313.2 3.1 late_z.1
  317.5 2.7 collective-permute-start.27
  320.6 2.1 collective-permute-done.26.refs_1_
  322.7 6.7 %collective-permute-done.27.refs_2_ = bf16[240,256]{1,0:T(8,128)(2,1)S(1)} collective-permute-done((bf16[240,256]{1,0:T(8,128)(2,1)}, bf16[240,256]{1,0:T(8,128)(2,1)S(1)}, u32[]{:S(2)}, u32[]{:S(2)}) %collective-permute-start.27) | collective-permute-done | bytes 122912 | tf_op jit(solution)/shard_map/ppermute | solution.py:676
  341.9 3.6 final.1
  349.4 5.6 %assemble.1 = (f32[128,4096]{1,0:T(8,128)}, f32[128,1024]{1,0:T(8,128)}, f32[128,3072]{1,0:T(8,128)}, f32[4,128,1024]{2,1,0:T(8,128)}) custom-call(s32[3]{0:T(128)} %pad_add_fusion.refs_0_.place_ref, bf16[128,3072]{1,0:T(8,128)(2,1)} %copy-done.1, bf16[128,3072]{1,0:T(8,128)(2,1)} %copy-done.6, bf16[128,3072]{1,0:T(8,128)(2,1)} %copy-done.7, ...), custom_call_target="tpu_custom_call" | custom-call | flops 58982 | bytes 353894 | tf_op jit(solution)/shard_map/assemble/pallas_call | solution.py:685
  (175 shorter events, 73.9 us)
Async XLA Ops:
  7.2 271.0 %reduce-scatter.3.cloned.1.call-start = ((), (), s32[]{:S(2)}) async-start(), calls=%async_computation.2 | async-start | bytes 5242880 | tf_op jit(solution)/shard_map/reduce_scatter | solution.py:978
  76.7 12.3 %collective-permute-start.3 = (bf16[512,256]{1,0:T(8,128)(2,1)S(1)}, bf16[512,256]{1,0:T(8,128)(2,1)S(1)}, u32[]{:S(2)}, u32[]{:S(2)}) collective-permute-start(bf16[512,256]{1,0:T(8,128)(2,1)S(1)} %copy-done.8), channel_id=1, source_target_pairs={{0,8},{8,0},{16,24},{24,16},{1,9},{9,1},{17,25},{25,17},{2,10},{10... | collective-permute-start | bytes 786440 | tf_op jit(solution)/shard_map/ppermute | solution.py:673
  77.3 12.7 %collective-permute-start.4 = (bf16[512,256]{1,0:T(8,128)(2,1)S(1)}, bf16[512,256]{1,0:T(8,128)(2,1)S(1)}, u32[]{:S(2)}, u32[]{:S(2)}) collective-permute-start(bf16[512,256]{1,0:T(8,128)(2,1)S(1)} %copy-done.9), channel_id=1, source_target_pairs={{0,16},{8,24},{16,0},{24,8},{1,17},{9,25},{17,1},{25,9},{2,18},{10... | collective-permute-start | bytes 786440 | tf_op jit(solution)/shard_map/ppermute | solution.py:673
  78.8 11.2 %collective-permute-start.5 = (bf16[512,256]{1,0:T(8,128)(2,1)}, bf16[512,256]{1,0:T(8,128)(2,1)S(1)}, u32[]{:S(2)}, u32[]{:S(2)}) collective-permute-start(bf16[512,256]{1,0:T(8,128)(2,1)} %get-tuple-element.167.refs_14_.refs_10_), channel_id=1, source_target_pairs={{0,24},{8,16},{16,8},{24,0},{1,25},{9,17},{17,9},{25,1},{2,26},{10... | collective-permute-start | bytes 786440 | tf_op jit(solution)/shard_map/ppermute | solution.py:673
  123.0 12.2 %collective-permute-start.6 = (bf16[512,256]{1,0:T(8,128)(2,1)}, bf16[512,256]{1,0:T(8,128)(2,1)S(1)}, u32[]{:S(2)}, u32[]{:S(2)}) collective-permute-start(bf16[512,256]{1,0:T(8,128)(2,1)} %get-tuple-element.176), channel_id=1, source_target_pairs={{0,8},{8,0},{16,24},{24,16},{1,9},{9,1},{17,25},{25,17},{2,10},{10... | collective-permute-start | bytes 786440 | tf_op jit(solution)/shard_map/ppermute | solution.py:673
  123.8 11.6 %collective-permute-start.7 = (bf16[512,256]{1,0:T(8,128)(2,1)}, bf16[512,256]{1,0:T(8,128)(2,1)S(1)}, u32[]{:S(2)}, u32[]{:S(2)}) collective-permute-start(bf16[512,256]{1,0:T(8,128)(2,1)} %get-tuple-element.177), channel_id=1, source_target_pairs={{0,16},{8,24},{16,0},{24,8},{1,17},{9,25},{17,1},{25,9},{2,18},{10... | collective-permute-start | bytes 786440 | tf_op jit(solution)/shard_map/ppermute | solution.py:673
  125.3 10.0 %collective-permute-start.8 = (bf16[512,256]{1,0:T(8,128)(2,1)}, bf16[512,256]{1,0:T(8,128)(2,1)S(1)}, u32[]{:S(2)}, u32[]{:S(2)}) collective-permute-start(bf16[512,256]{1,0:T(8,128)(2,1)} %get-tuple-element.178), channel_id=1, source_target_pairs={{0,24},{8,16},{16,8},{24,0},{1,25},{9,17},{17,9},{25,1},{2,26},{10... | collective-permute-start | bytes 786440 | tf_op jit(solution)/shard_map/ppermute | solution.py:673
  135.4 9.1 %collective-permute-start.9 = (bf16[512,5120]{1,0:T(8,128)(2,1)}, bf16[512,5120]{1,0:T(8,128)(2,1)}, u32[]{:S(2)}, u32[]{:S(2)}) collective-permute-start(bf16[512,5120]{1,0:T(8,128)(2,1)} %send.1), channel_id=1, source_target_pairs={{0,1},{1,0},{2,3},{3,2},{4,5},{5,4},{6,7},{7,6},{8,9},{9,8},{10,11... | collective-permute-start | bytes 15728648 | tf_op jit(solution)/shard_map/ppermute | solution.py:679
  139.8 18.7 %collective-permute-start.10 = (bf16[2048,1024]{1,0:T(8,128)(2,1)}, bf16[2048,1024]{1,0:T(8,128)(2,1)S(1)}, u32[]{:S(2)}, u32[]{:S(2)}) collective-permute-start(bf16[2048,1024]{1,0:T(8,128)(2,1)} %convolution_convert_fusion), channel_id=1, source_target_pairs={{0,1},{1,0},{2,3},{3,2},{4,5},{5,4},{6,7},{7,6},{8,9},{9,8},{10,11... | collective-permute-start | bytes 12582920 | tf_op jit(solution)/shard_map/ppermute | solution.py:679
  162.1 141.6 %reduce-scatter.5.cloned.1.call-start = ((), (), s32[]{:S(2)}) async-start(), calls=%async_computation.3 | async-start | bytes 2621440 | tf_op jit(solution)/shard_map/reduce_scatter | solution.py:1046
  162.1 38.6 %collective-permute-start.11 = (bf16[512,768]{1,0:T(8,128)(2,1)}, bf16[512,768]{1,0:T(8,128)(2,1)S(1)}, u32[]{:S(2)}, u32[]{:S(2)}) collective-permute-start(bf16[512,768]{1,0:T(8,128)(2,1)} %get-tuple-element.209), channel_id=1, source_target_pairs={{0,8},{8,0},{16,24},{24,16},{1,9},{9,1},{17,25},{25,17},{2,10},{10... | collective-permute-start | bytes 2359304 | tf_op jit(solution)/shard_map/ppermute | solution.py:673
  163.4 38.3 %collective-permute-start.12 = (bf16[512,768]{1,0:T(8,128)(2,1)}, bf16[512,768]{1,0:T(8,128)(2,1)S(1)}, u32[]{:S(2)}, u32[]{:S(2)}) collective-permute-start(bf16[512,768]{1,0:T(8,128)(2,1)} %get-tuple-element.210), channel_id=1, source_target_pairs={{0,16},{8,24},{16,0},{24,8},{1,17},{9,25},{17,1},{25,9},{2,18},{10... | collective-permute-start | bytes 2359304 | tf_op jit(solution)/shard_map/ppermute | solution.py:673
  164.3 37.4 %collective-permute-start.13 = (bf16[512,768]{1,0:T(8,128)(2,1)}, bf16[512,768]{1,0:T(8,128)(2,1)}, u32[]{:S(2)}, u32[]{:S(2)}) collective-permute-start(bf16[512,768]{1,0:T(8,128)(2,1)} %get-tuple-element.211), channel_id=1, source_target_pairs={{0,24},{8,16},{16,8},{24,0},{1,25},{9,17},{17,9},{25,1},{2,26},{10... | collective-permute-start | bytes 2359304 | tf_op jit(solution)/shard_map/ppermute | solution.py:673
  198.1 39.9 %collective-permute-start.14 = (bf16[512,896]{1,0:T(8,128)(2,1)}, bf16[512,896]{1,0:T(8,128)(2,1)S(1)}, u32[]{:S(2)}, u32[]{:S(2)}) collective-permute-start(bf16[512,896]{1,0:T(8,128)(2,1)} %get-tuple-element.224), channel_id=1, source_target_pairs={{0,8},{8,0},{16,24},{24,16},{1,9},{9,1},{17,25},{25,17},{2,10},{10... | collective-permute-start | bytes 2752520 | tf_op jit(solution)/shard_map/ppermute | solution.py:673
  199.7 41.2 %collective-permute-start.15 = (bf16[512,896]{1,0:T(8,128)(2,1)}, bf16[512,896]{1,0:T(8,128)(2,1)S(1)}, u32[]{:S(2)}, u32[]{:S(2)}) collective-permute-start(bf16[512,896]{1,0:T(8,128)(2,1)} %get-tuple-element.225), channel_id=1, source_target_pairs={{0,16},{8,24},{16,0},{24,8},{1,17},{9,25},{17,1},{25,9},{2,18},{10... | collective-permute-start | bytes 2752520 | tf_op jit(solution)/shard_map/ppermute | solution.py:673
  200.7 40.2 %collective-permute-start.16 = (bf16[512,896]{1,0:T(8,128)(2,1)}, bf16[512,896]{1,0:T(8,128)(2,1)S(1)}, u32[]{:S(2)}, u32[]{:S(2)}) collective-permute-start(bf16[512,896]{1,0:T(8,128)(2,1)} %get-tuple-element.226), channel_id=1, source_target_pairs={{0,24},{8,16},{16,8},{24,0},{1,25},{9,17},{17,9},{25,1},{2,26},{10... | collective-permute-start | bytes 2752520 | tf_op jit(solution)/shard_map/ppermute | solution.py:673
  236.1 8.6 %collective-permute-start.21 = (bf16[512,384]{1,0:T(8,128)(2,1)S(1)}, bf16[512,384]{1,0:T(8,128)(2,1)S(1)}, u32[]{:S(2)}, u32[]{:S(2)}) collective-permute-start(bf16[512,384]{1,0:T(8,128)(2,1)S(1)} %convolution_convert_fusion.1), channel_id=1, source_target_pairs={{0,1},{1,0},{2,3},{3,2},{4,5},{5,4},{6,7},{7,6},{8,9},{9,8},{10,11... | collective-permute-start | bytes 1179656 | tf_op jit(solution)/shard_map/ppermute | solution.py:679
  240.9 12.3 %collective-permute-start.17 = (bf16[512,384]{1,0:T(8,128)(2,1)}, bf16[512,384]{1,0:T(8,128)(2,1)S(1)}, u32[]{:S(2)}, u32[]{:S(2)}) collective-permute-start(bf16[512,384]{1,0:T(8,128)(2,1)} %get-tuple-element.232), channel_id=1, source_target_pairs={{0,8},{8,0},{16,24},{24,16},{1,9},{9,1},{17,25},{25,17},{2,10},{10... | collective-permute-start | bytes 1179656 | tf_op jit(solution)/shard_map/ppermute | solution.py:673
  241.7 11.9 %collective-permute-start.18 = (bf16[512,384]{1,0:T(8,128)(2,1)}, bf16[512,384]{1,0:T(8,128)(2,1)S(1)}, u32[]{:S(2)}, u32[]{:S(2)}) collective-permute-start(bf16[512,384]{1,0:T(8,128)(2,1)} %get-tuple-element.233), channel_id=1, source_target_pairs={{0,16},{8,24},{16,0},{24,8},{1,17},{9,25},{17,1},{25,9},{2,18},{10... | collective-permute-start | bytes 1179656 | tf_op jit(solution)/shard_map/ppermute | solution.py:673
  243.1 16.3 %collective-permute-start.19 = (bf16[512,384]{1,0:T(8,128)(2,1)}, bf16[512,384]{1,0:T(8,128)(2,1)}, u32[]{:S(2)}, u32[]{:S(2)}) collective-permute-start(bf16[512,384]{1,0:T(8,128)(2,1)} %get-tuple-element.234), channel_id=1, source_target_pairs={{0,24},{8,16},{16,8},{24,0},{1,25},{9,17},{17,9},{25,1},{2,26},{10... | collective-permute-start | bytes 1179656 | tf_op jit(solution)/shard_map/ppermute | solution.py:673
  279.7 11.2 %collective-permute-start.31 = (bf16[128,1024]{1,0:T(8,128)(2,1)S(1)}, bf16[128,1024]{1,0:T(8,128)(2,1)S(1)}, u32[]{:S(2)}, u32[]{:S(2)}) collective-permute-start(bf16[128,1024]{1,0:T(8,128)(2,1)S(1)} %get-tuple-element.299), channel_id=1, source_target_pairs={{0,24},{8,16},{16,8},{24,0},{1,25},{9,17},{17,9},{25,1},{2,26},{10... | collective-permute-start | bytes 786440 | tf_op jit(solution)/shard_map/ppermute | solution.py:673
  281.7 13.3 %collective-permute-start.30 = (bf16[128,1024]{1,0:T(8,128)(2,1)S(1)}, bf16[128,1024]{1,0:T(8,128)(2,1)S(1)}, u32[]{:S(2)}, u32[]{:S(2)}) collective-permute-start(bf16[128,1024]{1,0:T(8,128)(2,1)S(1)} %get-tuple-element.300), channel_id=1, source_target_pairs={{0,16},{8,24},{16,0},{24,8},{1,17},{9,25},{17,1},{25,9},{2,18},{10... | collective-permute-start | bytes 786440 | tf_op jit(solution)/shard_map/ppermute | solution.py:673
  283.1 12.7 %collective-permute-start.29 = (bf16[128,1024]{1,0:T(8,128)(2,1)S(1)}, bf16[128,1024]{1,0:T(8,128)(2,1)}, u32[]{:S(2)}, u32[]{:S(2)}) collective-permute-start(bf16[128,1024]{1,0:T(8,128)(2,1)S(1)} %get-tuple-element.298), channel_id=1, source_target_pairs={{0,8},{8,0},{16,24},{24,16},{1,9},{9,1},{17,25},{25,17},{2,10},{10... | collective-permute-start | bytes 786440 | tf_op jit(solution)/shard_map/ppermute | solution.py:673
  288.4 15.2 %collective-permute-start.23 = (bf16[656,256]{1,0:T(8,128)(2,1)}, bf16[656,256]{1,0:T(8,128)(2,1)S(1)}, u32[]{:S(2)}, u32[]{:S(2)}) collective-permute-start(bf16[656,256]{1,0:T(8,128)(2,1)} %get-tuple-element.262), channel_id=1, source_target_pairs={{0,8},{8,0},{16,24},{24,16},{1,9},{9,1},{17,25},{25,17},{2,10},{10... | collective-permute-start | bytes 1007624 | tf_op jit(solution)/shard_map/ppermute | solution.py:673
  290.3 13.3 %collective-permute-start.24 = (bf16[656,256]{1,0:T(8,128)(2,1)}, bf16[656,256]{1,0:T(8,128)(2,1)S(1)}, u32[]{:S(2)}, u32[]{:S(2)}) collective-permute-start(bf16[656,256]{1,0:T(8,128)(2,1)} %get-tuple-element.263), channel_id=1, source_target_pairs={{0,16},{8,24},{16,0},{24,8},{1,17},{9,25},{17,1},{25,9},{2,18},{10... | collective-permute-start | bytes 1007624 | tf_op jit(solution)/shard_map/ppermute | solution.py:673
  290.9 18.5 %collective-permute-start.25 = (bf16[656,256]{1,0:T(8,128)(2,1)}, bf16[656,256]{1,0:T(8,128)(2,1)S(1)}, u32[]{:S(2)}, u32[]{:S(2)}) collective-permute-start(bf16[656,256]{1,0:T(8,128)(2,1)} %get-tuple-element.264), channel_id=1, source_target_pairs={{0,24},{8,16},{16,8},{24,0},{1,25},{9,17},{17,9},{25,1},{2,26},{10... | collective-permute-start | bytes 1007624 | tf_op jit(solution)/shard_map/ppermute | solution.py:673
  310.6 21.3 %collective-permute-start.32 = (bf16[128,3072]{1,0:T(8,128)(2,1)S(1)}, bf16[128,3072]{1,0:T(8,128)(2,1)S(1)}, u32[]{:S(2)}, u32[]{:S(2)}) collective-permute-start(bf16[128,3072]{1,0:T(8,128)(2,1)S(1)} %pad_maximum_fusion.1.refs_1_), channel_id=1, source_target_pairs={{0,8},{8,0},{16,24},{24,16},{1,9},{9,1},{17,25},{25,17},{2,10},{10... | collective-permute-start | bytes 2359304 | tf_op jit(solution)/shard_map/ppermute | solution.py:673
  312.6 19.3 %collective-permute-start.33 = (bf16[128,3072]{1,0:T(8,128)(2,1)S(1)}, bf16[128,3072]{1,0:T(8,128)(2,1)S(1)}, u32[]{:S(2)}, u32[]{:S(2)}) collective-permute-start(bf16[128,3072]{1,0:T(8,128)(2,1)S(1)} %pad_maximum_fusion.1.refs_1_), channel_id=1, source_target_pairs={{0,16},{8,24},{16,0},{24,8},{1,17},{9,25},{17,1},{25,9},{2,18},{10... | collective-permute-start | bytes 2359304 | tf_op jit(solution)/shard_map/ppermute | solution.py:673
  317.5 11.9 %collective-permute-start.27 = (bf16[240,256]{1,0:T(8,128)(2,1)}, bf16[240,256]{1,0:T(8,128)(2,1)S(1)}, u32[]{:S(2)}, u32[]{:S(2)}) collective-permute-start(bf16[240,256]{1,0:T(8,128)(2,1)} %get-tuple-element.273), channel_id=1, source_target_pairs={{0,4},{2,6},{4,0},{6,2},{1,5},{3,7},{5,1},{7,3},{8,12},{10,14},{12... | collective-permute-start | bytes 368648 | tf_op jit(solution)/shard_map/ppermute | solution.py:676
  320.2 9.2 %collective-permute-start.28 = (bf16[240,256]{1,0:T(8,128)(2,1)}, bf16[240,256]{1,0:T(8,128)(2,1)S(1)}, u32[]{:S(2)}, u32[]{:S(2)}) collective-permute-start(bf16[240,256]{1,0:T(8,128)(2,1)} %get-tuple-element.274), channel_id=1, source_target_pairs={{0,6},{2,4},{4,2},{6,0},{1,7},{3,5},{5,3},{7,1},{8,14},{10,12},{12... | collective-permute-start | bytes 368648 | tf_op jit(solution)/shard_map/ppermute | solution.py:676
  335.5 13.2 %collective-permute-start.37 = (bf16[128,1536]{1,0:T(8,128)(2,1)S(1)}, bf16[128,1536]{1,0:T(8,128)(2,1)S(1)}, u32[]{:S(2)}, u32[]{:S(2)}) collective-permute-start(bf16[128,1536]{1,0:T(8,128)(2,1)S(1)} %slice.40), channel_id=1, source_target_pairs={{0,16},{8,24},{16,0},{24,8},{1,17},{9,25},{17,1},{25,9},{2,18},{10... | collective-permute-start | bytes 1179656 | tf_op jit(solution)/shard_map/ppermute | solution.py:673
  337.4 11.3 %collective-permute-start.38 = (bf16[128,1536]{1,0:T(8,128)(2,1)S(1)}, bf16[128,1536]{1,0:T(8,128)(2,1)}, u32[]{:S(2)}, u32[]{:S(2)}) collective-permute-start(bf16[128,1536]{1,0:T(8,128)(2,1)S(1)} %slice.41), channel_id=1, source_target_pairs={{0,8},{8,0},{16,24},{24,16},{1,9},{9,1},{17,25},{25,17},{2,10},{10... | collective-permute-start | bytes 1179656 | tf_op jit(solution)/shard_map/ppermute | solution.py:673
  (47 other events, 340.7 us)
Sparse Core Ops, SparseCore 0:
  162.2 77.1 reduce-scatter.2
  259.5 44.0 reduce-scatter.4
